TPU v7x, 256 devices: a whole 4x4x8 slice. The times are simulated.
256 devices in a mesh: zone: 64 (over z, y, core), band: 4 (over x).
Axes of the slice: x: 4, y: 4, z: 8, core: 2. Of those that a mesh axis runs over, the one named last changes fastest.
Arguments:
- pixels: float32 [32768, 32, 128], P(('zone', 'band')), may hold values from -6 to 6
- inv_var: float32 [32768, 32, 128], P(('zone', 'band')), may hold values from 0.25 to 4
- tile_offset: float32 [2, 32768], P(None, ('zone', 'band')), may hold values from 12 to 116, as said below
- psf_amp: float32 [3, 32768], P(None, ('zone', 'band')), may hold values from 0.3 to 1
- psf_sigma: float32 [3, 32768], P(None, ('zone', 'band')), may hold values from 0.9 to 2
- tile_blob: int32 [32768], P(('zone', 'band')), may hold values from 0 to 4095, as said below
- tile_band: int32 [32768], P(('zone', 'band')), may hold values from 0 to 2
- source_pos: float32 [2, 32768], P(None, 'zone'), may hold values from -5.3 to 5.3
- edge_rows: int32 [8192], P('zone'), may hold values from 0 to 511, as said below
- blob_members: int32 [4096, 16], P('zone'), may hold values from 0 to 639, as said below
- sources_per_blob: int32 [4096], P('zone'), may hold values from 1 to 16, as said below
Outputs:
- fluxes: float32 [3, 32768], P(None, 'zone')
Inputs may be any that keep to these rules, and one draw needn't show every extreme that they name: `tile_blob`: blob b lies in zone b // 64. Of one device's 128 tiles at most 4 cover blobs of one zone, and in every draw some zone receives exactly 4 tiles from every device of each band group. `edge_rows`: per zone, 64 lower edge rows then 64 upper edge rows, local row numbers, all 128 distinct. `blob_members`: slots at or beyond the blob's count hold 0. Every source is the live member of exactly one blob: a zone's lower edge rows belong to blobs of the previous zone and its upper edge rows to blobs of the next zone, except the first zone's lower and the last zone's upper rows, which stay in their own zone; the first zone never names the first 64 entries, the last zone never the last 64. `sources_per_blob`: the counts of one zone sum to 512; in every zone some blob has 16. `tile_offset`: row offsets lie within 12 to 20.
All inputs are finite; a program needn't handle non-finite values.
Results may differ from a plain program's by a relative error of at most 0.0003.
Values sent between devices are 32-bit elements; how exact they have to be, the bound alone decides.
No kernel may reach another device: no remote copies, remote signals or barrier semaphores. Data moves between devices by JAX's collectives and lax.ppermute only.
A program may use at most 64 MiB of HBM per device.

v0:
```python
import jax
import jax.numpy as jnp
from jax import lax
from jax.sharding import PartitionSpec as P

FILTER_BANDS = 3
MAX_SOURCES = 16


HIGH = lax.Precision.HIGHEST
PRIOR = 1.0


def extended_2(block, sides, width):
    for axis, dim in sides:
        count = lax.axis_size(axis)
        forward = [(i, i + 1) for i in range(count - 1)]
        backward = [(target, source) for source, target in forward]
        low = lax.ppermute(
            lax.slice_in_dim(block, block.shape[dim] - width, None, axis=dim), axis, forward
        )
        high = lax.ppermute(lax.slice_in_dim(block, 0, width, axis=dim), axis, backward)
        block = jnp.concatenate([low, block, high], axis=dim)
    return block


def terms_per_tile(
    tile_image_pixels,
    tile_weight_pixels,
    pixel_shift,
    source_amplitude,
    profile_widths,
    source_location,
    slot_alive_flags,
):
    pixel_rows = jnp.arange(tile_image_pixels.shape[0]).astype(jnp.float32)
    pixel_cols = jnp.arange(tile_image_pixels.shape[1]).astype(jnp.float32)
    inverse_spread = 0.5 / (profile_widths * profile_widths)
    row_displacement = pixel_rows[None, :] - pixel_shift[0] - source_location[0][:, None]
    delta_col = pixel_cols[None, :] - pixel_shift[1] - source_location[1][:, None]
    row_profile = jnp.exp(
        -inverse_spread[None, :, None] * (row_displacement * row_displacement)[:, None, :]
    ) * (source_amplitude[None, :, None] * slot_alive_flags[:, None, None])
    profile_col = jnp.exp(-inverse_spread[None, :, None] * (delta_col * delta_col)[:, None, :])
    rendered = jnp.sum(row_profile[:, :, :, None] * profile_col[:, :, None, :], axis=1).reshape(
        row_profile.shape[0], -1
    )
    weighted = rendered * tile_weight_pixels.reshape(1, -1)
    normal = jnp.einsum("sp,tp->st", weighted, rendered, precision=HIGH)
    projected = jnp.einsum("sp,p->s", weighted, tile_image_pixels.reshape(-1), precision=HIGH)
    return (normal, projected)


def stacked_terms(
    image_stack,
    pixel_weights,
    pixel_shifts,
    source_amplitudes,
    profile_widths,
    source_locations,
    slot_alive_flags,
):

    def single_tile(packed):
        return terms_per_tile(*packed)

    return lax.map(
        single_tile,
        (
            image_stack,
            pixel_weights,
            pixel_shifts,
            source_amplitudes,
            profile_widths,
            source_locations,
            slot_alive_flags,
        ),
        batch_size=8,
    )


def send_index(tile_blob, zone_count, blob_device_table, capacity):
    dest_zone = tile_blob // blob_device_table
    onehot = (dest_zone[:, None] == jnp.arange(zone_count, dtype=jnp.int32)[None, :]).astype(
        jnp.int32
    )
    earlier = jnp.cumsum(onehot, axis=0) - onehot
    slot_index = jnp.sum(earlier * onehot, axis=1)
    return dest_zone * capacity + slot_index


def accumulate(normal, projected, labels, blob_device_table):
    target_code = labels[:, 0] * FILTER_BANDS + labels[:, 1]
    targets = jnp.arange(blob_device_table * FILTER_BANDS).astype(jnp.float32)
    selector = (target_code[:, None] == targets[None, :]).astype(jnp.float32)
    order_n = normal.shape[1]
    matrices = jnp.einsum(
        "nq,nm->qm", selector, normal.reshape(normal.shape[0], -1), precision=HIGH
    ).reshape(-1, order_n, order_n)
    vectors = jnp.einsum("nq,ns->qs", selector, projected, precision=HIGH)
    return (matrices, vectors)


def solve_blocks(normal, vector):
    order_n = normal.shape[1]
    matrix = jnp.transpose(normal, (1, 2, 0))
    source = jnp.transpose(vector)
    factor = {}
    for column in range(order_n):
        diagonal = matrix[column, column] + PRIOR
        for inner_k in range(column):
            diagonal = diagonal - factor[column, inner_k] * factor[column, inner_k]
        pivot_root = jnp.sqrt(diagonal)
        factor[column, column] = pivot_root
        for row_index in range(column + 1, order_n):
            entry_val = matrix[row_index, column]
            for inner_k in range(column):
                entry_val = entry_val - factor[row_index, inner_k] * factor[column, inner_k]
            factor[row_index, column] = entry_val / pivot_root
    forward = []
    for row_index in range(order_n):
        entry_val = source[row_index]
        for inner_k in range(row_index):
            entry_val = entry_val - factor[row_index, inner_k] * forward[inner_k]
        forward.append(entry_val / factor[row_index, row_index])
    result_rows = [None] * order_n
    for row_index in reversed(range(order_n)):
        entry_val = forward[row_index]
        for inner_k in range(row_index + 1, order_n):
            entry_val = entry_val - factor[inner_k, row_index] * result_rows[inner_k]
        result_rows[row_index] = entry_val / factor[row_index, row_index]
    return jnp.transpose(jnp.stack(result_rows))


def on_device(
    pixels,
    inv_var,
    tile_offset,
    psf_amp,
    psf_sigma,
    tile_blob,
    tile_band,
    source_pos,
    edge_rows,
    blob_members,
    sources_per_blob,
):
    zone_count = lax.axis_size("zone")
    blob_device_table = sources_per_blob.shape[0]
    src_dev = source_pos.shape[1]
    edge_width = edge_rows.shape[0] // 2
    tile_count = pixels.shape[0]
    capacity = max(2, (2 * tile_count + zone_count - 1) // zone_count)
    slots_all = zone_count * capacity
    lower_rows = edge_rows[:edge_width]
    upper_rows = edge_rows[edge_width:]
    rim_rows = jnp.concatenate([source_pos[:, lower_rows], source_pos[:, upper_rows]], axis=1)
    framed = extended_2(rim_rows, (("zone", 1),), edge_width)
    extended = jnp.concatenate(
        [framed[:, :edge_width], source_pos, framed[:, 3 * edge_width :]], axis=1
    )
    slot_alive_flags = (
        jnp.arange(MAX_SOURCES, dtype=jnp.int32)[None, :] < sources_per_blob[:, None]
    ).astype(jnp.float32)
    member_pos = jnp.transpose(extended[:, blob_members], (1, 0, 2))
    positions_flat = send_index(tile_blob, zone_count, blob_device_table, capacity)
    labels = jnp.stack(
        [(tile_blob % blob_device_table).astype(jnp.float32), tile_band.astype(jnp.float32)], axis=1
    )
    table_pos, table_live = (
        lax.all_gather(member_pos, "zone", axis=0, tiled=True),
        lax.all_gather(slot_alive_flags, "zone", axis=0, tiled=True),
    )
    tile_pos = table_pos[tile_blob]
    tile_live = table_live[tile_blob]
    normal_own, projected_own = stacked_terms(
        pixels, inv_var, tile_offset.T, psf_amp.T, psf_sigma.T, tile_pos, tile_live
    )
    normal_buf = (
        jnp.zeros((slots_all, MAX_SOURCES, MAX_SOURCES), jnp.float32)
        .at[positions_flat]
        .set(normal_own)
        .reshape(zone_count, capacity, MAX_SOURCES, MAX_SOURCES)
    )
    projected_buf = (
        jnp.zeros((slots_all, MAX_SOURCES), jnp.float32)
        .at[positions_flat]
        .set(projected_own)
        .reshape(zone_count, capacity, MAX_SOURCES)
    )
    labels_buf = (
        jnp.zeros((slots_all, 2), jnp.float32)
        .at[positions_flat]
        .set(labels)
        .reshape(zone_count, capacity, 2)
    )
    normal_got, projected_got, labels_got = (
        lax.all_to_all(normal_buf, "zone", split_axis=0, concat_axis=0, tiled=True),
        lax.all_to_all(projected_buf, "zone", split_axis=0, concat_axis=0, tiled=True),
        lax.all_to_all(labels_buf, "zone", split_axis=0, concat_axis=0, tiled=True),
    )
    items_got = normal_got.shape[0] * normal_got.shape[1]
    matrices, vectors = accumulate(
        normal_got.reshape(items_got, MAX_SOURCES, MAX_SOURCES),
        projected_got.reshape(items_got, MAX_SOURCES),
        labels_got.reshape(items_got, 2),
        blob_device_table,
    )
    matrices, vectors = lax.psum((matrices, vectors), "band")
    solved_fluxes = solve_blocks(matrices, vectors)
    value_entries = (
        solved_fluxes.reshape(blob_device_table, FILTER_BANDS, MAX_SOURCES)
        * slot_alive_flags[:, None, :]
    )
    spread = jnp.transpose(value_entries, (1, 0, 2)).reshape(FILTER_BANDS, -1)
    flux_ext = (
        jnp.zeros((FILTER_BANDS, src_dev + 2 * edge_width), jnp.float32)
        .at[:, blob_members.reshape(-1)]
        .add(spread)
    )
    rim_back = jnp.concatenate(
        [flux_ext[:, :edge_width], flux_ext[:, edge_width + src_dev :]], axis=1
    )
    returned = extended_2(rim_back, (("zone", 1),), edge_width)
    own_flux = flux_ext[:, edge_width : edge_width + src_dev]
    own_flux = own_flux.at[:, lower_rows].add(returned[:, :edge_width])
    own_flux = own_flux.at[:, upper_rows].add(returned[:, 3 * edge_width :])
    return own_flux


def solution(mesh):
    return jax.shard_map(
        on_device,
        mesh=mesh,
        in_specs=(
            P(("zone", "band"), None, None),
            P(("zone", "band"), None, None),
            P(None, ("zone", "band")),
            P(None, ("zone", "band")),
            P(None, ("zone", "band")),
            P(("zone", "band")),
            P(("zone", "band")),
            P(None, "zone"),
            P("zone"),
            P("zone", None),
            P("zone"),
        ),
        out_specs=P(None, "zone"),
        check_vma=False,
    )
```

profile of v0, /device:TPU:25, one launch (start us, length us, event | category | flops | bytes accessed | tf_op | source)
XLA Modules:
  0.0 493.7 jit_solution(12673679470210379359)
XLA Ops:
  8.8 3.8 collective-permute-start
  19.0 12.8 %all-to-all-start = ((f32[64,4,2]{1,2,0:T(2,128)}), f32[64,4,2]{1,2,0:T(2,128)S(1)}, u32[]{:S(2)}, u32[]{:S(2)}) async-start(f32[64,4,2]{1,2,0:T(2,128)} %copy.105), calls=%async_computation | async-start | bytes 131072 | tf_op jit(solution)/shard_map/all_to_all | solution.py:200
  34.2 50.1 %all-gather = f32[64,64,16]{1,2,0:T(8,128)S(1)} all-gather(f32[1,64,16]{1,2,0:T(8,128)S(1)} %get-tuple-element.775), channel_id=1, replica_groups=mesh['zone'=64,'band'=4] {'zone'}, dimensions={0}, use_global_device_ids=true | all-gather | bytes 266240 | tf_op jit(solution)/shard_map/all_gather | solution.py:172
  89.2 55.1 %all_gather.6 = f32[4096,2,16]{2,1,0:T(2,128)} all-gather(f32[64,2,16]{2,1,0:T(2,128)S(1)} %bitcast.1785), channel_id=1, replica_groups=mesh['zone'=64,'band'=4] {'zone'}, dimensions={0}, use_global_device_ids=true | all-gather | bytes 532480 | tf_op jit(solution)/shard_map/all_gather | solution.py:171
  147.3 210.3 %while.12 = (s32[]{:T(128)}, f32[16,8,16,16]{3,2,1,0:T(8,128)S(1)}, f32[16,8,16]{2,1,0:T(8,128)S(1)}, f32[16,8,3]{1,0,2:T(8,128)S(1)}, f32[16,8,2]{1,0,2:T(8,128...) while((s32[]{:T(128)}, f32[16,8,16,16]{3,2,1,0:T(8,128)S(1)}, ...), condition=%wide.region_5.6_spmd, body=%wide.region_3.5_spmd.sunk | while | flops 110741352 | bytes 14517353 | solution.py:67
  148.4 3.5 multiply_reduce_fusion.2
  161.5 3.5 multiply_reduce_fusion.2
  174.7 3.5 multiply_reduce_fusion.2
  187.8 3.5 multiply_reduce_fusion.2
  200.9 3.5 multiply_reduce_fusion.2
  214.1 3.5 multiply_reduce_fusion.2
  227.2 3.5 multiply_reduce_fusion.2
  240.4 3.5 multiply_reduce_fusion.2
  253.5 3.5 multiply_reduce_fusion.2
  266.6 3.5 multiply_reduce_fusion.2
  279.8 3.5 multiply_reduce_fusion.2
  359.3 8.9 %all-to-all-start.1 = ((f32[64,4,16]{2,1,0:T(4,128)}), f32[64,4,16]{2,1,0:T(4,128)S(1)}, u32[]{:S(2)}, u32[]{:S(2)}) async-start(f32[64,4,16]{2,1,0:T(4,128)} %bitcast.30), calls=%async_computation.1 | async-start | bytes 262144 | tf_op jit(solution)/shard_map/all_to_all | solution.py:199
  368.4 4.3 scatter_fusion
  376.9 7.6 %all-to-all-start.2 = ((f32[64,1,1024]{2,1,0:T(1,128)}), f32[64,1,1024]{2,1,0:T(1,128)S(1)}, u32[]{:S(2)}, u32[]{:S(2)}) async-start(f32[64,1,1024]{2,1,0:T(1,128)} %reshape.21178), calls=%async_computation.2 | async-start | bytes 524288 | tf_op jit(solution)/shard_map/all_to_all | solution.py:198
  385.0 14.1 %psum.14 = f32[16,192]{1,0:T(8,128)S(1)} all-reduce(f32[16,192]{1,0:T(8,128)S(1)} %fusion.15), channel_id=1, replica_groups=mesh['zone'=64,'band'=4] {'band'}, use_global_device_ids=true, to_apply=%region_7.8 | all-reduce | flops 3072 | bytes 24576 | tf_op jit(solution)/shard_map/psum | solution.py:209
  403.8 46.3 %all-reduce.2.cloned.1.call-done = f32[16,16,192]{2,1,0:T(8,128)} async-done(((f32[16,16,192]{2,1,0:T(8,128)}), f32[16,16,192]{2,1,0:T(8,128)}) %all-reduce.2.cloned.1.call-update) | async-done | bytes 196624 | tf_op jit(solution)/shard_map/psum | solution.py:209
  465.8 6.1 %scatter_custom_fusion.3 = f32[3,640]{0,1:T(8,128)S(1)} fusion(s32[1024]{0:T(1024)S(1)} %bitcast.1957, f32[1024,3]{1,0:T(8,128)S(1)} %copy.111, f32[]{:T(128)} %constant.43.clone.1), kind=kCustom, calls=%fused_computation.53 | custom fusion | flops 3072 | bytes 7684 | tf_op jit(solution)/shard_map/scatter-add | solution.py:219
  472.0 5.8 %collective-permute-start.2 = (f32[3,64]{0,1:T(8,128)S(1)}, f32[3,64]{0,1:T(8,128)S(1)}, u32[]{:S(2)}, u32[]{:S(2)}) collective-permute-start(f32[3,64]{0,1:T(8,128)S(1)} %get-tuple-element.621), channel_id=1, source_target_pairs={{0,4},{4,8},{8,12},{12,16},{16,20},{20,24},{24,28},{28,32},{32,36}... | collective-permute-start | bytes 2312 | tf_op jit(solution)/shard_map/ppermute | solution.py:19
  480.9 4.2 collective-permute-done.3
  (536 shorter events, 220.6 us)
Async XLA Ops:
  7.3 8.4 %copy-start.2 = (s32[64]{0:T(128)}, s32[64]{0:T(128)S(1)}, u32[]{:S(2)}) copy-start(s32[64]{0:T(128)S(1)} %get-tuple-element.780) | copy-start | bytes 772
  8.2 76.7 %copy-start.3 = (f32[3,128]{1,0:T(4,128)S(1)}, f32[3,128]{1,0:T(4,128)}, u32[]{:S(2)}) copy-start(f32[3,128]{1,0:T(4,128)} %param.17) | copy-start | bytes 4612
  8.2 76.8 %copy-start.4 = (f32[3,128]{1,0:T(4,128)S(1)}, f32[3,128]{1,0:T(4,128)}, u32[]{:S(2)}) copy-start(f32[3,128]{1,0:T(4,128)} %param.16) | copy-start | bytes 4612
  8.8 77.1 %collective-permute-start = (f32[2,64]{0,1:T(8,128)S(1)}, f32[2,64]{0,1:T(8,128)S(1)}, u32[]{:S(2)}, u32[]{:S(2)}) collective-permute-start(f32[2,64]{0,1:T(8,128)S(1)} %bitcast.1961), channel_id=1, source_target_pairs={{0,4},{4,8},{8,12},{12,16},{16,20},{20,24},{24,28},{28,32},{32,36}... | collective-permute-start | bytes 1544 | tf_op jit(solution)/shard_map/ppermute | solution.py:19
  13.2 71.9 %copy-start.5 = (f32[2,128]{1,0:T(2,128)S(1)}, f32[2,128]{1,0:T(2,128)}, u32[]{:S(2)}) copy-start(f32[2,128]{1,0:T(2,128)} %param.15) | copy-start | bytes 3076
  13.2 72.7 %collective-permute-start.1 = (f32[2,64]{0,1:T(8,128)S(1)}, f32[2,64]{0,1:T(8,128)S(1)}, u32[]{:S(2)}, u32[]{:S(2)}) collective-permute-start(f32[2,64]{0,1:T(8,128)S(1)} %bitcast.1962), channel_id=1, source_target_pairs={{4,0},{8,4},{12,8},{16,12},{20,16},{24,20},{28,24},{32,28},{36,32}... | collective-permute-start | bytes 1544 | tf_op jit(solution)/shard_map/ppermute | solution.py:22
  16.2 68.8 %copy-start.6 = (s32[128]{0:T(128)}, s32[128]{0:T(128)S(1)}, u32[]{:S(2)}) copy-start(s32[128]{0:T(128)S(1)} %compare_select_fusion.4) | copy-start | bytes 1540
  19.0 340.2 %all-to-all-start = ((f32[64,4,2]{1,2,0:T(2,128)}), f32[64,4,2]{1,2,0:T(2,128)S(1)}, u32[]{:S(2)}, u32[]{:S(2)}) async-start(f32[64,4,2]{1,2,0:T(2,128)} %copy.105), calls=%async_computation | async-start | bytes 131072 | tf_op jit(solution)/shard_map/all_to_all | solution.py:200
  89.2 58.1 %copy-start = (f32[16,8,16,16]{3,2,1,0:T(8,128)S(1)}, f32[16,8,16,16]{3,2,1,0:T(8,128)}, u32[]{:S(2)}) copy-start(f32[16,8,16,16]{3,2,1,0:T(8,128)} %custom-call.10) | copy-start | bytes 393220
  357.6 10.8 %copy-start.7 = (s32[128]{0:T(128)S(1)}, s32[128]{0:T(128)}, u32[]{:S(2)}) copy-start(s32[128]{0:T(128)} %copy-done.6) | copy-start | bytes 1540
  359.3 17.6 %all-to-all-start.1 = ((f32[64,4,16]{2,1,0:T(4,128)}), f32[64,4,16]{2,1,0:T(4,128)S(1)}, u32[]{:S(2)}, u32[]{:S(2)}) async-start(f32[64,4,16]{2,1,0:T(4,128)} %bitcast.30), calls=%async_computation.1 | async-start | bytes 262144 | tf_op jit(solution)/shard_map/all_to_all | solution.py:199
  376.9 22.2 %all-to-all-start.2 = ((f32[64,1,1024]{2,1,0:T(1,128)}), f32[64,1,1024]{2,1,0:T(1,128)S(1)}, u32[]{:S(2)}, u32[]{:S(2)}) async-start(f32[64,1,1024]{2,1,0:T(1,128)} %reshape.21178), calls=%async_computation.2 | async-start | bytes 524288 | tf_op jit(solution)/shard_map/all_to_all | solution.py:198
  384.5 65.6 %all-reduce.2.cloned.1.call-start = ((), (), s32[]{:S(2)}) async-start(), calls=%async_computation.3 | async-start | bytes 524288 | tf_op jit(solution)/shard_map/psum | solution.py:209
  450.0 13.4 %copy-start.1 = (f32[16,16,192]{2,1,0:T(8,128)S(1)}, f32[16,16,192]{2,1,0:T(8,128)}, u32[]{:S(2)}) copy-start(f32[16,16,192]{2,1,0:T(8,128)} %all-reduce.2.cloned.1.call-done) | copy-start | bytes 589828
  472.0 7.8 %collective-permute-start.2 = (f32[3,64]{0,1:T(8,128)S(1)}, f32[3,64]{0,1:T(8,128)S(1)}, u32[]{:S(2)}, u32[]{:S(2)}) collective-permute-start(f32[3,64]{0,1:T(8,128)S(1)} %get-tuple-element.621), channel_id=1, source_target_pairs={{0,4},{4,8},{8,12},{12,16},{16,20},{20,24},{24,28},{28,32},{32,36}... | collective-permute-start | bytes 2312 | tf_op jit(solution)/shard_map/ppermute | solution.py:19
  477.8 7.3 %collective-permute-start.3 = (f32[3,64]{0,1:T(8,128)S(1)}, f32[3,64]{0,1:T(8,128)S(1)}, u32[]{:S(2)}, u32[]{:S(2)}) collective-permute-start(f32[3,64]{0,1:T(8,128)S(1)} %get-tuple-element.620), channel_id=1, source_target_pairs={{4,0},{8,4},{12,8},{16,12},{20,16},{24,20},{28,24},{32,28},{36,32}... | collective-permute-start | bytes 2312 | tf_op jit(solution)/shard_map/ppermute | solution.py:22
Sparse Core Ops, SparseCore 0:
  403.9 46.1 all-reduce.1
where the time goes:
time: 497 us; the launch traced here: 494 us
  blocking collectives  119 us (24%)
  other arithmetic  96.7 us (19%)
  matrix products  93.2 us (19%)
  local copies, waits for them, and re-layouts  72.9 us (15%)
  waiting for transfers between devices  53.3 us (11%)
  starting transfers between devices  42.7 us (9%)
  between operations  13.9 us (3%)
    reduce_sum x16, other arithmetic, terms_per_tile(): jnp.sum(row_profile[:, :, :, None] * profile_col[:, :, None, :], axis=1)  55.9 us
    all_gather x1, blocking collectives, on_device(): lax.all_gather(member_pos, 'zone', axis=0, tiled=True)  55.1 us
    dot_general x16, matrix products, terms_per_tile(): normal = jnp.einsum('sp,tp->st', weighted, rendered, precision=HIGH)  50.5 us
    all_gather x1, blocking collectives, on_device(): lax.all_gather(slot_alive_flags, 'zone', axis=0, tiled=True)  50.1 us
    psum x1, waiting for transfers between devices, on_device(): matrices, vectors = lax.psum((matrices, vectors), 'band')  46.3 us
    dot_general x16, matrix products, terms_per_tile(): jnp.einsum('sp,p->s', weighted, tile_image_pixels.reshape(-1), precision=...  41.3 us
    reshape x16, local copies, waits for them, and re-layouts, terms_per_tile(): jnp.sum(row_profile[:, :, :, None] * profile_col[:, :, None, :], axis=1)  27.9 us
    dynamic_slice x112, local copies, waits for them, and re-layouts, stacked_terms(): lax.map(single_tile, (image_stack, pixel_weights, pixel_shifts, source_am...  17.8 us
  transfers between devices with their start and end apart: 8, of which 3 were waited for; matrix products, arithmetic and copies ran while one was open for 47% of the time, Pallas kernels for 0%

commit v1 on v0

v1 whole, which is shorter than its diff:
```python
import functools

import jax
import jax.numpy as jnp
from jax import lax
from jax.experimental import pallas as pl
from jax.experimental.pallas import tpu as pltpu
from jax.sharding import PartitionSpec as P

BANDS = 3
SLOTS = 16
PH = 32
PW = 128
SRC = 512
BLOBS = 64
EDGE = 64
GROUP = 8
TABLE_ROWS = 16
MARK = 1000.0
LOG2E = 1.4426950408889634
F32 = jnp.float32
BF16 = jnp.bfloat16
NT = (((1,), (1,)), ((), ()))
NN = (((1,), (0,)), ((), ()))
TN = (((0,), (0,)), ((), ()))
VMEM = pl.BlockSpec(memory_space=pltpu.VMEM)
SMEM = pl.BlockSpec(memory_space=pltpu.SMEM)


def iota(shape, axis):
    return lax.broadcasted_iota(jnp.int32, shape, axis)


def three_parts(x):
    high = x.astype(BF16)
    rest = x - high.astype(F32)
    mid = rest.astype(BF16)
    low = (rest - mid.astype(F32)).astype(BF16)
    return high, mid, low


def dot(a, b, dims):
    return lax.dot_general(a, b, dims, preferred_element_type=F32)


def exact_left(x, onehot, dims):
    high, mid, low = three_parts(x)
    return (dot(low, onehot, dims) + dot(mid, onehot, dims)) + dot(high, onehot, dims)


def table_kernel(members, counts, source_pos, edge_rows, out):
    cnt = counts[...]
    above = iota((BLOBS, BLOBS), 0)
    beside = iota((BLOBS, BLOBS), 1)
    spread = jnp.broadcast_to(cnt, (BLOBS, BLOBS))
    start = jnp.sum(jnp.where(beside < above, spread, 0.0), axis=1, keepdims=True)
    own = jnp.sum(jnp.where(beside == above, spread, 0.0), axis=1, keepdims=True)
    start_row = jnp.sum(jnp.where(above == beside, start, 0.0), axis=0, keepdims=True)
    entry = iota((BLOBS, SRC), 1).astype(F32)
    inside = jnp.logical_and(entry >= start, entry < start + own)
    slot = jnp.sum(jnp.where(inside, entry - start, 0.0), axis=0, keepdims=True)
    picked = exact_left(members[...].astype(F32), inside.astype(BF16), TN)
    slot_ids = iota((SLOTS, SRC), 0).astype(F32)
    source = jnp.sum(jnp.where(slot_ids == slot, picked, 0.0), axis=0, keepdims=True)
    wanted = jnp.concatenate([source, edge_rows[...].astype(F32) + float(EDGE)], axis=1)
    width = SRC + 2 * EDGE
    row_ids = iota((SRC, width), 0).astype(F32) + float(EDGE)
    onehot = jnp.where(row_ids == wanted, 1.0, 0.0).astype(BF16)
    pos = jnp.concatenate([source_pos[...], jnp.zeros((6, SRC), F32)], axis=0)
    got = exact_left(pos, onehot, NN)
    lanes = iota((1, width), 1)
    mark = jnp.where(wanted < float(EDGE), wanted + (MARK + EDGE), wanted + (MARK - EDGE - SRC))
    outside = jnp.logical_or(wanted < float(EDGE), wanted >= float(EDGE + SRC))
    marked = jnp.logical_and(lanes < SRC, outside)
    got = jnp.where(marked, mark, got)
    rows = [got[p : p + 1, PW * n : PW * (n + 1)] for p in range(2) for n in range(4)]
    rows += [got[p : p + 1, SRC : SRC + PW] for p in range(2)]
    rows.append(jnp.concatenate([start_row, cnt], axis=1))
    rows.append(jnp.zeros((TABLE_ROWS - 11, PW), F32))
    table = jnp.concatenate(rows, axis=0)

    def write(z, _):
        out[z] = table
        return 0

    lax.fori_loop(0, out.shape[0], write, 0, unroll=8)


def tile_kernel(
    blob_s,
    band_s,
    off_s,
    amp_s,
    inv_s,
    table,
    pixels,
    weights,
    out,
    buf_a,
    buf_b,
    roots,
    full,
    info,
    ranges,
    used,
):
    zones = table.shape[0]
    tiles = pixels.shape[0] // PH
    lane = iota((8, PW), 1)
    sub = iota((8, PW), 0)
    lane16 = iota((SLOTS, PW), 1).astype(F32)
    slot_f = iota((SLOTS, PW), 0).astype(F32)
    spot = lane >> 4
    entry = lane & (SLOTS - 1)

    def clear(z, _):
        out[z] = jnp.zeros((8, PW), F32)
        used[z] = 0
        return 0

    lax.fori_loop(0, zones, clear, 0)

    def patch(z, _):
        before = jnp.maximum(z - 1, 0)
        after = jnp.minimum(z + 1, zones - 1)
        value = table[z, 0:8, :]
        sides = []
        for row in (8, 9):
            low = jnp.broadcast_to(table[before, row : row + 1, :], (8, PW))
            high = jnp.broadcast_to(table[after, row : row + 1, :], (8, PW))
            sides.append(jnp.where(lane < EDGE, high, low))
        edges = jnp.where(sub < 4, sides[0], sides[1])
        at = jnp.clip(value.astype(jnp.int32) - int(MARK), 0, PW - 1)
        found = jnp.take_along_axis(edges, at, axis=1, mode="promise_in_bounds")
        full[z] = jnp.where(value >= MARK, found, value)
        return 0

    lax.fori_loop(0, zones, patch, 0, unroll=4)

    def pick(t, _):
        blob = blob_s[0, t]
        row = table[blob >> 6, 10:11, :]
        info[pl.ds(t, 1), :] = jnp.where((lane[0:1] & (BLOBS - 1)) == (blob & (BLOBS - 1)), row, 0.0)
        return 0

    lax.fori_loop(0, tiles, pick, 0, unroll=8)
    half = iota((PW, 2 * PW), 0) // BLOBS == iota((PW, 2 * PW), 1) // PW
    ranges[...] = exact_left(info[...], jnp.where(half, 1.0, 0.0).astype(BF16), NN)
    ones = jnp.ones((PW, PW), BF16)

    def positions(g):
        picked = [[], []]
        spans = ranges[pl.ds(pl.multiple_of(g * GROUP, GROUP), GROUP), :]
        for s in range(GROUP):
            t = g * GROUP + s
            zone = blob_s[0, t] >> 6
            start = jnp.broadcast_to(spans[s : s + 1, 0:PW], (SLOTS, PW))
            index = start + slot_f
            hits = [index == lane16 + float(PW * n) for n in range(4)]
            for p in range(2):
                value = jnp.zeros((SLOTS, PW), F32)
                for n in range(4):
                    row = full[zone, 4 * p + n : 4 * p + n + 1, :]
                    value = jnp.where(hits[n], jnp.broadcast_to(row, (SLOTS, PW)), value)
                picked[p].append(value)
        return exact_left(jnp.concatenate(picked[0] + picked[1], axis=0), ones, NN), spans

    def render(g, buf):
        base = g * (GROUP * PH)
        where, spans = positions(g)
        for i in range(PH):
            root = jnp.sqrt(weights[pl.ds(base + i, GROUP, stride=PH), :])
            roots[GROUP * i : GROUP * (i + 1), :] = root
            scaled = root * pixels[pl.ds(base + i, GROUP, stride=PH), :]
            high = scaled.astype(BF16).astype(F32)
            both = jnp.concatenate([high, scaled - high], axis=0)
            buf[256:272, PW * i : PW * (i + 1)] = both.astype(BF16)
        for s in range(GROUP):
            t = g * GROUP + s
            y = where[SLOTS * s : SLOTS * (s + 1)]
            x = where[128 + SLOTS * s : 128 + SLOTS * (s + 1)]
            count = jnp.broadcast_to(spans[s : s + 1, PW : 2 * PW], (SLOTS, PW))
            live = jnp.where(slot_f < count, 1.0, 0.0)
            dx = (lane16 - off_s[1, t]) - x
            dx = dx * dx
            scales = [inv_s[c, t] for c in range(3)]
            cols = [jnp.exp2(scales[c] * dx) * (live * amp_s[c, t]) for c in range(3)]
            for i in range(PH):
                dy = (float(i) - off_s[0, t]) - y
                dy = dy * dy
                total = None
                for c in range(3):
                    term = jnp.exp2(scales[c] * dy) * cols[c]
                    total = term if total is None else total + term
                row = GROUP * i + s
                total = total * jnp.broadcast_to(roots[row : row + 1, :], (SLOTS, PW))
                high = total.astype(BF16)
                low = (total - high.astype(F32)).astype(BF16)
                buf[SLOTS * s : SLOTS * (s + 1), PW * i : PW * (i + 1)] = low
                buf[128 + SLOTS * s : 128 + SLOTS * (s + 1), PW * i : PW * (i + 1)] = high

    def finish(g, buf):
        prod = dot(buf[128:272, :], buf[0:256, :], NT)
        cross = prod[0:128, 0:128]
        gram = prod[0:128, 128:256] + (cross + jnp.transpose(cross))
        rhs8 = prod[128:136, 128:256] + (prod[128:136, 0:128] + prod[136:144, 128:256])
        upper = jnp.zeros((8, PW), F32)
        lower = jnp.zeros((8, PW), F32)
        for s in range(GROUP):
            upper = jnp.where(spot == s, gram[SLOTS * s : SLOTS * s + 8], upper)
            lower = jnp.where(spot == s, gram[SLOTS * s + 8 : SLOTS * s + 16], lower)
        fold = jnp.where(entry < sub, pltpu.roll(lower, PW - 8, 1), upper)
        diag = jnp.sum(jnp.where(entry == sub + 8, lower, 0.0), axis=0, keepdims=True)
        rhs = jnp.sum(jnp.where(spot == sub, rhs8, 0.0), axis=0, keepdims=True)
        label = jnp.zeros((1, PW), F32)
        for s in range(GROUP):
            t = g * GROUP + s
            code = band_s[0, t] * BLOBS + (blob_s[0, t] & (BLOBS - 1)) + 1
            label = jnp.where(lane[0:1] == SLOTS * s, code.astype(F32), label)
        extra = jnp.where(sub == 0, rhs, jnp.where(sub == 1, diag + label, 0.0))
        for s in range(GROUP):
            t = g * GROUP + s
            zone = blob_s[0, t] >> 6
            place = used[zone]
            used[zone] = place + 1
            shift = SLOTS * (place - s)
            value = jnp.where(
                lane < 64,
                pltpu.roll(fold, (shift + 128) & 127, 1),
                pltpu.roll(extra, (shift + 192) & 127, 1),
            )
            mine = (spot & 3) == place
            out[zone] = jnp.where(mine, value, out[zone])

    groups = tiles // GROUP
    render(0, buf_a)

    def step(n, _):
        render(2 * n + 1, buf_b)
        finish(2 * n, buf_a)
        render(jnp.minimum(2 * n + 2, groups - 1), buf_a)
        finish(2 * n + 1, buf_b)
        return 0

    lax.fori_loop(0, groups // 2, step, 0)


def gather_kernel(got, out):
    zones = got.shape[0] // 8
    lane = iota((zones, PW), 1)
    spot = lane >> 4
    parts = [got[pl.ds(r, zones, stride=8), :] for r in range(8)]
    body = []
    for s in range(4):
        main = jnp.zeros((zones, PW), F32)
        for r in range(8):
            shift = (SLOTS * (r - s)) % PW
            moved = pltpu.roll(parts[r], shift, 1) if shift else parts[r]
            main = jnp.where(spot == r, moved, main)
        rhs = pltpu.roll(parts[0], (64 - SLOTS * s) % PW, 1)
        rest = pltpu.roll(parts[1], (64 + SLOTS - SLOTS * s) % PW, 1)
        extra = jnp.where(spot == 0, rhs, jnp.where(spot == 1, rest, 0.0))
        body.append(jnp.concatenate([main, extra], axis=1))
    values = jnp.concatenate(body, axis=0)
    label = values[:, PW + SLOTS : PW + SLOTS + 1]
    systems = out.shape[1]
    codes = iota((4 * zones, systems), 1).astype(F32) + 1.0
    onehot = jnp.where(label == codes, 1.0, 0.0).astype(BF16)
    total = exact_left(values, onehot, TN)
    out[...] = total[0 : out.shape[0]]


def solve_kernel(first, second, third, fourth, members, counts, own, before, after, left, right, xs):
    sums = (first[...] + second[...]) + (third[...] + fourth[...])
    width = sums.shape[1]
    left[...] = sums[:, 0:PW]
    right[...] = sums[:, PW:width]
    sub = iota((8, width), 0)

    def bcast(x, k):
        return jnp.broadcast_to(x[k : k + 1], (8, width))

    low_half = [None] * SLOTS
    high_half = [None] * SLOTS
    for k in range(8):
        low_half[k] = sums[SLOTS * k : SLOTS * k + 8, :] + jnp.where(sub == k, 1.0, 0.0)
        high_half[k] = sums[SLOTS * k + 8 : SLOTS * k + 16, :]
        corner = jnp.concatenate(
            [half[pl.ds(k, 8, stride=SLOTS), :] for half in (left, right)], axis=1
        )
        diag = bcast(sums[128 + SLOTS + 8 : 128 + SLOTS + 16, :], k) + 1.0
        high_half[8 + k] = jnp.where(sub == k, diag, corner)
    rhs = [sums[128:136, :], sums[136:144, :]]
    pivots = []
    values = []
    for k in range(SLOTS):
        halves = [low_half[k], high_half[k]] if k < 8 else [None, high_half[k]]
        inverse = 1.0 / bcast(halves[k // 8], k % 8)
        scaled = [None if h is None else h * inverse for h in halves]
        value = bcast(rhs[k // 8], k % 8)
        pivots.append(inverse)
        values.append(value)
        for h in range(2):
            if scaled[h] is not None:
                rhs[h] = rhs[h] - scaled[h] * value
        for j in range(k + 1, SLOTS):
            factor = bcast(scaled[j // 8], j % 8)
            if j < 8:
                low_half[j] = low_half[j] - factor * halves[0]
            high_half[j] = high_half[j] - factor * halves[1]
    x = [jnp.zeros((8, width), F32), jnp.zeros((8, width), F32)]
    for k in reversed(range(SLOTS)):
        acc = jnp.where(sub > k - 8, high_half[k] * x[1], 0.0)
        if k < 8:
            acc = acc + jnp.where(sub > k, low_half[k] * x[0], 0.0)
        solved = (values[k] - jnp.sum(acc, axis=0, keepdims=True)) * pivots[k]
        x[k // 8] = jnp.where(sub == k % 8, solved, x[k // 8])
    xs[0:8, :] = x[0]
    xs[8:16, :] = x[1]

    lane = iota((8, PW), 1)
    sub8 = iota((8, PW), 0)
    doubled = []
    for k in range(BANDS):
        tile = xs[:, PW * (k // 2) : PW * (k // 2 + 1)]
        turned = pltpu.roll(tile, 64, 1)
        wide = iota((SLOTS, PW), 1)
        doubled.append(
            jnp.where(wide < 64, tile, turned) if k % 2 == 0 else jnp.where(wide < 64, turned, tile)
        )
    pieces = []
    for n in range(8):
        piece = jnp.zeros((8, PW), F32)
        for k in range(BANDS):
            row = jnp.where(
                lane < 64,
                jnp.broadcast_to(doubled[k][2 * n : 2 * n + 1], (8, PW)),
                jnp.broadcast_to(doubled[k][2 * n + 1 : 2 * n + 2], (8, PW)),
            )
            piece = jnp.where(sub8 == k, row, piece)
        pieces.append(piece)
    flat = jnp.concatenate(pieces, axis=1)
    extent = SRC + 2 * EDGE
    columns = members[...].astype(F32)
    slots = iota((BLOBS, SLOTS), 1).astype(F32)
    columns = jnp.where(slots < counts[...], columns, -1.0)
    targets = iota((BLOBS, extent), 1)
    targets = jnp.where(targets < SRC, targets + EDGE, jnp.where(targets < SRC + EDGE, targets - SRC, targets))
    targets = targets.astype(F32)
    onehot = jnp.concatenate(
        [jnp.where(columns[:, j : j + 1] == targets, 1.0, 0.0).astype(BF16) for j in range(SLOTS)],
        axis=0,
    )
    fluxes = exact_left(flat, onehot, NN)
    own[...] = fluxes[:, 0:SRC]
    rim = fluxes[:, SRC:extent]
    before[...] = jnp.where(lane < EDGE, rim, 0.0)
    after[...] = jnp.where(lane < EDGE, 0.0, rim)


def edge_kernel(own, from_before, from_after, edge_rows, out):
    rim = pltpu.roll(from_before[...] + from_after[...], EDGE, 1)
    rows = edge_rows[...]
    targets = iota((2 * EDGE, SRC), 1)
    onehot = jnp.where(rows == targets, 1.0, 0.0).astype(BF16)
    out[...] = (own[...] + exact_left(rim, onehot, NN))[0:BANDS]


def call(kernel, out_shape, in_specs, scratch=(), out_specs=None):
    return pl.pallas_call(
        kernel,
        out_shape=out_shape,
        in_specs=in_specs,
        out_specs=VMEM if out_specs is None else out_specs,
        scratch_shapes=list(scratch),
        compiler_params=pltpu.CompilerParams(vmem_limit_bytes=48 * 1024 * 1024),
    )


def on_device(
    pixels,
    inv_var,
    tile_offset,
    psf_amp,
    psf_sigma,
    tile_blob,
    tile_band,
    source_pos,
    edge_rows,
    blob_members,
    sources_per_blob,
):
    zones = lax.axis_size("zone")
    bands = lax.axis_size("band")
    shape = jax.ShapeDtypeStruct
    counts = sources_per_blob.astype(F32)
    spread = call(table_kernel, shape((zones, TABLE_ROWS, PW), F32), [VMEM] * 4)(
        blob_members, counts.reshape(1, -1), source_pos, edge_rows.reshape(1, -1)
    )
    table = lax.all_to_all(spread, "zone", split_axis=0, concat_axis=0, tiled=True)
    inverse = -LOG2E * (0.5 / (psf_sigma * psf_sigma))
    tiles = pixels.shape[0]
    terms = call(
        tile_kernel,
        shape((zones, 8, PW), F32),
        [SMEM] * 5 + [VMEM] * 3,
        [
            pltpu.VMEM((272, PH * PW), BF16),
            pltpu.VMEM((272, PH * PW), BF16),
            pltpu.VMEM((GROUP * PH, PW), F32),
            pltpu.VMEM((zones, 8, PW), F32),
            pltpu.VMEM((tiles, PW), F32),
            pltpu.VMEM((tiles, 2 * PW), F32),
            pltpu.SMEM((zones,), jnp.int32),
        ],
    )(
        tile_blob.reshape(1, -1),
        tile_band.reshape(1, -1),
        tile_offset,
        psf_amp,
        inverse,
        table,
        pixels.reshape(tiles * PH, PW),
        inv_var.reshape(tiles * PH, PW),
    )
    got = lax.all_to_all(terms, "zone", split_axis=0, concat_axis=0, tiled=True)
    systems = call(gather_kernel, shape((160, 2 * PW), F32), [VMEM])(got.reshape(zones * 8, PW))
    others = [
        lax.ppermute(systems, "band", [(i, (i + k) % bands) for i in range(bands)])
        for k in range(1, bands)
    ]
    own, before, after = call(
        solve_kernel,
        (shape((8, SRC), F32), shape((8, PW), F32), shape((8, PW), F32)),
        [VMEM] * 6,
        [pltpu.VMEM((160, PW), F32), pltpu.VMEM((160, PW), F32), pltpu.VMEM((SLOTS, 2 * PW), F32)],
        (VMEM, VMEM, VMEM),
    )(systems, *others, blob_members, counts.reshape(-1, 1))
    up = [(i, i + 1) for i in range(zones - 1)]
    down = [(b, a) for a, b in up]
    from_before = lax.ppermute(after, "zone", up)
    from_after = lax.ppermute(before, "zone", down)
    return call(edge_kernel, shape((BANDS, SRC), F32), [VMEM] * 4)(
        own, from_before, from_after, edge_rows.reshape(-1, 1)
    )


def solution(mesh):
    tile = P(("zone", "band"))
    return jax.shard_map(
        on_device,
        mesh=mesh,
        in_specs=(
            P(("zone", "band"), None, None),
            P(("zone", "band"), None, None),
            P(None, ("zone", "band")),
            P(None, ("zone", "band")),
            P(None, ("zone", "band")),
            tile,
            tile,
            P(None, "zone"),
            P("zone"),
            P("zone", None),
            P("zone"),
        ),
        out_specs=P(None, "zone"),
        check_vma=False,
    )
```

time: 497 us -> 123 us (0.25)
  blocking collectives: 119 us -> 18.1 us
  other arithmetic: 96.7 us -> 1.35 us
  matrix products: 93.2 us -> 0 us
  local copies, waits for them, and re-layouts: 72.9 us -> 8.18 us
  Pallas kernels: 0 us -> 43.6 us
  waiting for transfers between devices: 53.3 us -> 25 us
  starting transfers between devices: 42.7 us -> 26.4 us
  between operations: 13.9 us -> 0.07 us
    all_gather x2 -> x0, blocking collectives: 105 us -> none  [the longest x1 55.1 us: on_device(): lax.all_gather(member_pos, 'zone', axis=0, tiled=True)]
    dot_general x34 -> x0, matrix products: 93.2 us -> none  [the longest x16 50.5 us: terms_per_tile(): normal = jnp.einsum('sp,tp->st', weighted, rendered, precision=HIGH)]
    reduce_sum x17 -> x0, other arithmetic: 56 us -> none  [the longest x16 55.9 us: terms_per_tile(): jnp.sum(row_profile[:, :, :, None] * profile_col[:, :, None, :], axis=1)]
    psum x1 -> x0, waiting for transfers between devices: 46.3 us -> none  [on_device(): matrices, vectors = lax.psum((matrices, vectors), 'band')]
    pallas_call x0 -> x5, Pallas kernels: none -> 43.6 us  [the longest x1 39.4 us: on_device(): call(tile_kernel, shape((zones, 8, PW), F32), [SMEM] * 5 + [VMEM] * 3, [p...]
    reshape x25 -> x2, local copies, waits for them, and re-layouts: 29.8 us -> 0.21 us  [the longest x1 0.11 us: on_device(): edge_rows.reshape(-1, 1)]
    all_to_all x0 -> x1, blocking collectives: none -> 18.1 us  [on_device(): got = lax.all_to_all(terms, 'zone', split_axis=0, concat_axis=0, tiled=True)]
    dynamic_slice x112 -> x0, local copies, waits for them, and re-layouts: 17.8 us -> none  [stacked_terms(): lax.map(single_tile, (image_stack, pixel_weights, pixel_shifts, source_am...]
  transfers between devices with their start and end apart: 8 -> 6, of which waited for: 3 -> 4; matrix products, arithmetic and copies ran while one was open for 47% -> 1% of each run, Pallas kernels for 0% -> 0%
where the time goes in v1:
time: 123 us
  Pallas kernels  43.6 us (35%)
  starting transfers between devices  26.4 us (21%)
  waiting for transfers between devices  25 us (20%)
  blocking collectives  18.1 us (15%)
  local copies, waits for them, and re-layouts  8.18 us (7%)
  other arithmetic  1.35 us (1%)
    pallas_call x1, Pallas kernels, on_device(): call(tile_kernel, shape((zones, 8, PW), F32), [SMEM] * 5 + [VMEM] * 3, [p...  39.4 us
    all_to_all x1, blocking collectives, on_device(): got = lax.all_to_all(terms, 'zone', split_axis=0, concat_axis=0, tiled=True)  18.1 us
    all_to_all x1, waiting for transfers between devices, on_device(): lax.all_to_all(spread, 'zone', split_axis=0, concat_axis=0, tiled=True)  15.3 us
    all_to_all x1, starting transfers between devices, on_device(): lax.all_to_all(spread, 'zone', split_axis=0, concat_axis=0, tiled=True)  12.2 us
    unnamed x19, local copies, waits for them, and re-layouts  7.97 us
    ppermute x1, starting transfers between devices, on_device(): from_before = lax.ppermute(after, 'zone', up)  7.36 us
    ppermute x1, waiting for transfers between devices, on_device(): from_after = lax.ppermute(before, 'zone', down)  4.98 us
    ppermute x3, starting transfers between devices, on_device(): lax.ppermute(systems, 'band', [(i, (i + k) % bands) for i in range(bands)])  4.9 us
  transfers between devices with their start and end apart: 6, of which 4 were waited for; matrix products, arithmetic and copies ran while one was open for 1% of the time, Pallas kernels for 0%

profile of v1, /device:TPU:25, one launch (start us, length us, event | category | flops | bytes accessed | tf_op | source)
XLA Modules:
  0.0 122.7 jit_solution(14169919163192166637)
XLA Ops:
  0.0 0.8 copy.12.members
  0.8 0.7 convert_bitcast_fusion
  1.4 0.7 copy-done.2
  2.1 0.7 copy-done.4
  2.8 1.5 %shard_map.109 = f32[64,16,128]{2,1,0:T(8,128)} custom-call(s32[64,16]{1,0:T(8,128)S(1)} %copy.12.members, f32[1,64]{1,0:T(1,128)S(1)} %get-tuple-element.12.counts, f32[2,512]{1,0:T(2,128)S(1)} %copy-done.2, s32[1,128]{1,0:T(1,128)S(1)} %bitcast.14), custom_call_target="tpu_custom_call" | custom-call | tf_op jit(solution)/shard_map/pallas_call | solution.py:397
  4.3 12.2 %all-to-all-start = ((f32[64,16,128]{2,1,0:T(8,128)}), f32[64,16,128]{2,1,0:T(8,128)S(1)}, u32[]{:S(2)}, u32[]{:S(2)}) async-start(f32[64,16,128]{2,1,0:T(8,128)} %shard_map.109), calls=%async_computation | async-start | bytes 1048576 | tf_op jit(solution)/shard_map/all_to_all | solution.py:400
  16.5 0.7 divide_multiply_fusion.inv_s
  17.2 15.3 %all-to-all-done.table = f32[64,16,128]{2,1,0:T(8,128)S(1)} async-done(((f32[64,16,128]{2,1,0:T(8,128)}), f32[64,16,128]{2,1,0:T(8,128)S(1)}, u32[]{:S(2)}, u32[]{:S(2)}) %all-to-all-start) | async-done | bytes 524320 | tf_op jit(solution)/shard_map/all_to_all | solution.py:400
  32.5 1.6 %copy-done = f32[128,32,128]{2,1,0:T(8,128)S(1)} copy-done((f32[128,32,128]{2,1,0:T(8,128)S(1)}, f32[128,32,128]{2,1,0:T(8,128)}, u32[]{:S(2)}) %copy-start) | copy-done | bytes 2097176
  34.1 1.6 %copy-done.1 = f32[128,32,128]{2,1,0:T(8,128)S(1)} copy-done((f32[128,32,128]{2,1,0:T(8,128)S(1)}, f32[128,32,128]{2,1,0:T(8,128)}, u32[]{:S(2)}) %copy-start.1) | copy-done | bytes 2097176
  35.7 0.7 copy-done.3
  36.4 0.7 copy-done.6
  38.4 39.4 %shard_map.110 = f32[64,8,128]{2,1,0:T(8,128)S(1)} custom-call(s32[1,128]{1,0:T(1,128)S(1)} %bitcast.16, s32[1,128]{1,0:T(1,128)S(1)} %bitcast.17, f32[2,128]{1,0:T(2,128)S(1)} %copy-done.6, f32[3,128]{1,0:T(4,128)S(1)} %copy-done.3, f32[3,128]{1,0:T(4,128)S(1)} %divide_multiply_fusion.inv_s, f32[64,16,128]{2,1,0:T(8,128)S(1)} %all-to-all-done.table, ...), custom_call_target="tpu_custom_call" | custom-call | tf_op jit(solution)/shard_map/pallas_call | solution.py:403
  77.8 18.1 %all_to_all.10 = f32[64,8,128]{2,1,0:T(8,128)S(1)} all-to-all(f32[64,8,128]{2,1,0:T(8,128)S(1)} %shard_map.110), channel_id=1, replica_groups=mesh['zone'=64,'band'=4] {'zone'}, dimensions={0} | all-to-all | bytes 524288 | tf_op jit(solution)/shard_map/all_to_all | solution.py:426
  95.9 0.7 shard_map.111.first
  96.6 1.3 %collective-permute-start = (f32[160,256]{1,0:T(8,128)S(1)}, f32[160,256]{1,0:T(8,128)S(1)}, u32[]{:S(2)}, u32[]{:S(2)}) collective-permute-start(f32[160,256]{1,0:T(8,128)S(1)} %shard_map.111.first), channel_id=1, source_target_pairs={{0,1},{1,2},{2,3},{3,0},{4,5},{5,6},{6,7},{7,4},{8,9},{9,10},{10,1... | collective-permute-start | bytes 491528 | tf_op jit(solution)/shard_map/ppermute | solution.py:429
  97.9 2.4 %collective-permute-start.1 = (f32[160,256]{1,0:T(8,128)S(1)}, f32[160,256]{1,0:T(8,128)S(1)}, u32[]{:S(2)}, u32[]{:S(2)}) collective-permute-start(f32[160,256]{1,0:T(8,128)S(1)} %shard_map.111.first), channel_id=1, source_target_pairs={{0,2},{1,3},{2,0},{3,1},{4,6},{5,7},{6,4},{7,5},{8,10},{9,11},{10,... | collective-permute-start | bytes 491528 | tf_op jit(solution)/shard_map/ppermute | solution.py:429
  100.3 1.2 collective-permute-start.2
  102.0 4.2 %collective-permute-done.1.third = f32[160,256]{1,0:T(8,128)S(1)} collective-permute-done((f32[160,256]{1,0:T(8,128)S(1)}, f32[160,256]{1,0:T(8,128)S(1)}, u32[]{:S(2)}, u32[]{:S(2)}) %collective-permute-start.1) | collective-permute-done | bytes 163872 | tf_op jit(solution)/shard_map/ppermute | solution.py:429
  106.3 1.2 shard_map.112
  107.4 7.4 %collective-permute-start.3 = (f32[8,128]{1,0:T(8,128)S(1)}, f32[8,128]{1,0:T(8,128)S(1)}, u32[]{:S(2)}, u32[]{:S(2)}) collective-permute-start(f32[8,128]{1,0:T(8,128)S(1)} %get-tuple-element.9), channel_id=1, source_target_pairs={{0,4},{4,8},{8,12},{12,16},{16,20},{20,24},{24,28},{28,32},{32,36}... | collective-permute-start | bytes 12296 | tf_op jit(solution)/shard_map/ppermute | solution.py:441
  114.8 1.9 %collective-permute-start.4 = (f32[8,128]{1,0:T(8,128)S(1)}, f32[8,128]{1,0:T(8,128)S(1)}, u32[]{:S(2)}, u32[]{:S(2)}) collective-permute-start(f32[8,128]{1,0:T(8,128)S(1)} %get-tuple-element.10), channel_id=1, source_target_pairs={{4,0},{8,4},{12,8},{16,12},{20,16},{24,20},{28,24},{32,28},{36,32}... | collective-permute-start | bytes 12296 | tf_op jit(solution)/shard_map/ppermute | solution.py:442
  116.8 5.0 %collective-permute-done.4.from_after = f32[8,128]{1,0:T(8,128)S(1)} collective-permute-done((f32[8,128]{1,0:T(8,128)S(1)}, f32[8,128]{1,0:T(8,128)S(1)}, u32[]{:S(2)}, u32[]{:S(2)}) %collective-permute-start.4) | collective-permute-done | bytes 4128 | tf_op jit(solution)/shard_map/ppermute | solution.py:442
  121.8 0.8 shard_map.113
  (17 shorter events, 2.0 us)
Async XLA Ops:
  1.4 0.7 copy-start.2
  2.1 0.7 copy-start.4
  4.3 28.2 %all-to-all-start = ((f32[64,16,128]{2,1,0:T(8,128)}), f32[64,16,128]{2,1,0:T(8,128)S(1)}, u32[]{:S(2)}, u32[]{:S(2)}) async-start(f32[64,16,128]{2,1,0:T(8,128)} %shard_map.109), calls=%async_computation | async-start | bytes 1048576 | tf_op jit(solution)/shard_map/all_to_all | solution.py:400
  32.5 1.6 %copy-start = (f32[128,32,128]{2,1,0:T(8,128)S(1)}, f32[128,32,128]{2,1,0:T(8,128)}, u32[]{:S(2)}) copy-start(f32[128,32,128]{2,1,0:T(8,128)} %param.11) | copy-start | bytes 6291460
  34.1 1.6 %copy-start.1 = (f32[128,32,128]{2,1,0:T(8,128)S(1)}, f32[128,32,128]{2,1,0:T(8,128)}, u32[]{:S(2)}) copy-start(f32[128,32,128]{2,1,0:T(8,128)} %param.12) | copy-start | bytes 6291460
  35.7 0.7 copy-start.3
  36.4 0.7 copy-start.6
  37.1 0.7 copy-start.7
  37.7 0.7 copy-start.8
  38.4 78.4 %copy-start.5 = (s32[128]{0:T(128)S(1)}, s32[128]{0:T(128)}, u32[]{:S(2)}) copy-start(s32[128]{0:T(128)} %param.19) | copy-start | bytes 1540
  96.6 5.5 %collective-permute-start = (f32[160,256]{1,0:T(8,128)S(1)}, f32[160,256]{1,0:T(8,128)S(1)}, u32[]{:S(2)}, u32[]{:S(2)}) collective-permute-start(f32[160,256]{1,0:T(8,128)S(1)} %shard_map.111.first), channel_id=1, source_target_pairs={{0,1},{1,2},{2,3},{3,0},{4,5},{5,6},{6,7},{7,4},{8,9},{9,10},{10,1... | collective-permute-start | bytes 491528 | tf_op jit(solution)/shard_map/ppermute | solution.py:429
  97.9 8.4 %collective-permute-start.1 = (f32[160,256]{1,0:T(8,128)S(1)}, f32[160,256]{1,0:T(8,128)S(1)}, u32[]{:S(2)}, u32[]{:S(2)}) collective-permute-start(f32[160,256]{1,0:T(8,128)S(1)} %shard_map.111.first), channel_id=1, source_target_pairs={{0,2},{1,3},{2,0},{3,1},{4,6},{5,7},{6,4},{7,5},{8,10},{9,11},{10,... | collective-permute-start | bytes 491528 | tf_op jit(solution)/shard_map/ppermute | solution.py:429
  100.3 6.0 %collective-permute-start.2 = (f32[160,256]{1,0:T(8,128)S(1)}, f32[160,256]{1,0:T(8,128)S(1)}, u32[]{:S(2)}, u32[]{:S(2)}) collective-permute-start(f32[160,256]{1,0:T(8,128)S(1)} %shard_map.111.first), channel_id=1, source_target_pairs={{0,3},{1,0},{2,1},{3,2},{4,7},{5,4},{6,5},{7,6},{8,11},{9,8},{10,9... | collective-permute-start | bytes 491528 | tf_op jit(solution)/shard_map/ppermute | solution.py:429
  107.4 9.4 %collective-permute-start.3 = (f32[8,128]{1,0:T(8,128)S(1)}, f32[8,128]{1,0:T(8,128)S(1)}, u32[]{:S(2)}, u32[]{:S(2)}) collective-permute-start(f32[8,128]{1,0:T(8,128)S(1)} %get-tuple-element.9), channel_id=1, source_target_pairs={{0,4},{4,8},{8,12},{12,16},{16,20},{20,24},{24,28},{28,32},{32,36}... | collective-permute-start | bytes 12296 | tf_op jit(solution)/shard_map/ppermute | solution.py:441
  114.8 7.0 %collective-permute-start.4 = (f32[8,128]{1,0:T(8,128)S(1)}, f32[8,128]{1,0:T(8,128)S(1)}, u32[]{:S(2)}, u32[]{:S(2)}) collective-permute-start(f32[8,128]{1,0:T(8,128)S(1)} %get-tuple-element.10), channel_id=1, source_target_pairs={{4,0},{8,4},{12,8},{16,12},{20,16},{24,20},{28,24},{32,28},{36,32}... | collective-permute-start | bytes 12296 | tf_op jit(solution)/shard_map/ppermute | solution.py:442

commit v2 on v1

--- a/solution.py
+++ b/solution.py
@@ -49,7 +49,7 @@
 
 
 def table_kernel(members, counts, source_pos, edge_rows, out):
-    cnt = counts[...]
+    cnt = counts[...].astype(F32)
     above = iota((BLOBS, BLOBS), 0)
     beside = iota((BLOBS, BLOBS), 1)
     spread = jnp.broadcast_to(cnt, (BLOBS, BLOBS))
@@ -59,7 +59,7 @@
     entry = iota((BLOBS, SRC), 1).astype(F32)
     inside = jnp.logical_and(entry >= start, entry < start + own)
     slot = jnp.sum(jnp.where(inside, entry - start, 0.0), axis=0, keepdims=True)
-    picked = exact_left(members[...].astype(F32), inside.astype(BF16), TN)
+    picked = exact_left(members[...].astype(F32), inside.astype(BF16), NN)
     slot_ids = iota((SLOTS, SRC), 0).astype(F32)
     source = jnp.sum(jnp.where(slot_ids == slot, picked, 0.0), axis=0, keepdims=True)
     wanted = jnp.concatenate([source, edge_rows[...].astype(F32) + float(EDGE)], axis=1)
@@ -86,39 +86,28 @@
     lax.fori_loop(0, out.shape[0], write, 0, unroll=8)
 
 
-def tile_kernel(
-    blob_s,
-    band_s,
-    off_s,
-    amp_s,
-    inv_s,
-    table,
-    pixels,
-    weights,
-    out,
-    buf_a,
-    buf_b,
-    roots,
-    full,
-    info,
-    ranges,
-    used,
-):
+def prepare_kernel(pixels, weights, roots, scaled):
+    def group(g, _):
+        base = pl.multiple_of(g * (GROUP * PH), GROUP * PH)
+        for i in range(PH):
+            root = jnp.sqrt(weights[pl.ds(base + i, GROUP, stride=PH), :])
+            roots[pl.ds(base + GROUP * i, GROUP), :] = root
+            product = root * pixels[pl.ds(base + i, GROUP, stride=PH), :]
+            high = product.astype(BF16).astype(F32)
+            both = jnp.concatenate([high, product - high], axis=0)
+            scaled[g, i // 2, :, PW * (i % 2) : PW * (i % 2 + 1)] = both.astype(BF16)
+        return 0
+
+    lax.fori_loop(0, scaled.shape[0], group, 0)
+
+
+def place_kernel(code_s, table, places, counts, full, info, ranges):
     zones = table.shape[0]
-    tiles = pixels.shape[0] // PH
+    tiles = info.shape[0]
     lane = iota((8, PW), 1)
     sub = iota((8, PW), 0)
     lane16 = iota((SLOTS, PW), 1).astype(F32)
     slot_f = iota((SLOTS, PW), 0).astype(F32)
-    spot = lane >> 4
-    entry = lane & (SLOTS - 1)
-
-    def clear(z, _):
-        out[z] = jnp.zeros((8, PW), F32)
-        used[z] = 0
-        return 0
-
-    lax.fori_loop(0, zones, clear, 0)
 
     def patch(z, _):
         before = jnp.maximum(z - 1, 0)
@@ -135,25 +124,26 @@
         full[z] = jnp.where(value >= MARK, found, value)
         return 0
 
-    lax.fori_loop(0, zones, patch, 0, unroll=4)
+    lax.fori_loop(0, zones, patch, 0, unroll=8)
 
     def pick(t, _):
-        blob = blob_s[0, t]
+        blob = code_s[0, t] >> 2
         row = table[blob >> 6, 10:11, :]
         info[pl.ds(t, 1), :] = jnp.where((lane[0:1] & (BLOBS - 1)) == (blob & (BLOBS - 1)), row, 0.0)
         return 0
 
-    lax.fori_loop(0, tiles, pick, 0, unroll=8)
+    lax.fori_loop(0, tiles, pick, 0, unroll=16)
     half = iota((PW, 2 * PW), 0) // BLOBS == iota((PW, 2 * PW), 1) // PW
     ranges[...] = exact_left(info[...], jnp.where(half, 1.0, 0.0).astype(BF16), NN)
+    counts[...] = ranges[:, PW : 2 * PW]
     ones = jnp.ones((PW, PW), BF16)
 
-    def positions(g):
+    def positions(g, _):
         picked = [[], []]
         spans = ranges[pl.ds(pl.multiple_of(g * GROUP, GROUP), GROUP), :]
         for s in range(GROUP):
             t = g * GROUP + s
-            zone = blob_s[0, t] >> 6
+            zone = code_s[0, t] >> 8
             start = jnp.broadcast_to(spans[s : s + 1, 0:PW], (SLOTS, PW))
             index = start + slot_f
             hits = [index == lane16 + float(PW * n) for n in range(4)]
@@ -163,47 +153,89 @@
                     row = full[zone, 4 * p + n : 4 * p + n + 1, :]
                     value = jnp.where(hits[n], jnp.broadcast_to(row, (SLOTS, PW)), value)
                 picked[p].append(value)
-        return exact_left(jnp.concatenate(picked[0] + picked[1], axis=0), ones, NN), spans
-
-    def render(g, buf):
-        base = g * (GROUP * PH)
-        where, spans = positions(g)
-        for i in range(PH):
-            root = jnp.sqrt(weights[pl.ds(base + i, GROUP, stride=PH), :])
-            roots[GROUP * i : GROUP * (i + 1), :] = root
-            scaled = root * pixels[pl.ds(base + i, GROUP, stride=PH), :]
-            high = scaled.astype(BF16).astype(F32)
-            both = jnp.concatenate([high, scaled - high], axis=0)
-            buf[256:272, PW * i : PW * (i + 1)] = both.astype(BF16)
-        for s in range(GROUP):
-            t = g * GROUP + s
-            y = where[SLOTS * s : SLOTS * (s + 1)]
-            x = where[128 + SLOTS * s : 128 + SLOTS * (s + 1)]
-            count = jnp.broadcast_to(spans[s : s + 1, PW : 2 * PW], (SLOTS, PW))
-            live = jnp.where(slot_f < count, 1.0, 0.0)
-            dx = (lane16 - off_s[1, t]) - x
-            dx = dx * dx
-            scales = [inv_s[c, t] for c in range(3)]
-            cols = [jnp.exp2(scales[c] * dx) * (live * amp_s[c, t]) for c in range(3)]
-            for i in range(PH):
-                dy = (float(i) - off_s[0, t]) - y
-                dy = dy * dy
-                total = None
+        places[g] = exact_left(jnp.concatenate(picked[0] + picked[1], axis=0), ones, NN)
+        return 0
+
+    lax.fori_loop(0, tiles // GROUP, positions, 0, unroll=2)
+
+
+def tile_kernel(
+    code_s,
+    par_s,
+    places,
+    counts,
+    roots,
+    scaled,
+    out,
+    buf_a,
+    buf_b,
+    used,
+):
+    zones = out.shape[0]
+    tiles = counts.shape[0]
+    lane = iota((8, PW), 1)
+    sub = iota((8, PW), 0)
+    lane16 = iota((SLOTS, PW), 1).astype(F32)
+    slot_f = iota((SLOTS, PW), 0).astype(F32)
+    spot = lane >> 4
+    entry = lane & (SLOTS - 1)
+
+    def clear(z, _):
+        out[z] = jnp.zeros((8, PW), F32)
+        used[z] = 0
+        return 0
+
+    lax.fori_loop(0, zones, clear, 0)
+
+    def store(g, buf, s, i, total):
+        root = roots[pl.ds(GROUP * (PH * g + i) + s, 1), :]
+        total = total * jnp.broadcast_to(root, (SLOTS, PW))
+        high = total.astype(BF16)
+        low = (total - high.astype(F32)).astype(BF16)
+        first = pl.multiple_of(SLOTS * s, SLOTS)
+        side = slice(PW * (i % 2), PW * (i % 2 + 1))
+        buf[i // 2, pl.ds(first, SLOTS), side] = low
+        buf[i // 2, pl.ds(128 + first, SLOTS), side] = high
+
+    def render(g, s, buf, meanwhile):
+        t = g * GROUP + s
+        first = pl.multiple_of(SLOTS * s, SLOTS)
+        y = places[g, pl.ds(first, SLOTS), :]
+        x = places[g, pl.ds(128 + first, SLOTS), :]
+        count = jnp.broadcast_to(counts[pl.ds(t, 1), :], (SLOTS, PW))
+        live = jnp.where(slot_f < count, 1.0, 0.0)
+        dx = (lane16 - par_s[1, t]) - x
+        dx = dx * dx
+        dy = (float(PH // 2) - par_s[0, t]) - y
+        flat = jnp.zeros((8, PW), F32)
+        here, up, down, turn = [], [], [], []
+        for c in range(3):
+            scale = par_s[5 + c, t]
+            col = jnp.exp2(scale * dx) * (live * par_s[2 + c, t])
+            here.append(jnp.exp2(scale * (dy * dy)) * col)
+            up.append(jnp.exp2(scale * (2.0 * dy + 1.0)))
+            down.append(jnp.exp2(scale * (1.0 - 2.0 * dy)))
+            step = jnp.exp2(flat + 2.0 * scale)
+            turn.append(jnp.concatenate([step, step], axis=0))
+        store(g, buf, s, PH // 2, (here[0] + here[1]) + here[2])
+        above, below = list(here), list(here)
+        for n in range(1, PH // 2 + 1):
+            if n in meanwhile:
+                meanwhile[n]()
+            for c in range(3):
+                below[c] = below[c] * down[c]
+                down[c] = down[c] * turn[c]
+            store(g, buf, s, PH // 2 - n, (below[0] + below[1]) + below[2])
+            if n < PH // 2:
                 for c in range(3):
-                    term = jnp.exp2(scales[c] * dy) * cols[c]
-                    total = term if total is None else total + term
-                row = GROUP * i + s
-                total = total * jnp.broadcast_to(roots[row : row + 1, :], (SLOTS, PW))
-                high = total.astype(BF16)
-                low = (total - high.astype(F32)).astype(BF16)
-                buf[SLOTS * s : SLOTS * (s + 1), PW * i : PW * (i + 1)] = low
-                buf[128 + SLOTS * s : 128 + SLOTS * (s + 1), PW * i : PW * (i + 1)] = high
-
-    def finish(g, buf):
-        prod = dot(buf[128:272, :], buf[0:256, :], NT)
+                    above[c] = above[c] * up[c]
+                    up[c] = up[c] * turn[c]
+                store(g, buf, s, PH // 2 + n, (above[0] + above[1]) + above[2])
+
+    def finish(g, prod, sides):
         cross = prod[0:128, 0:128]
         gram = prod[0:128, 128:256] + (cross + jnp.transpose(cross))
-        rhs8 = prod[128:136, 128:256] + (prod[128:136, 0:128] + prod[136:144, 128:256])
+        rhs8 = sides[0:8, 128:256] + (sides[0:8, 0:128] + sides[8:16, 128:256])
         upper = jnp.zeros((8, PW), F32)
         lower = jnp.zeros((8, PW), F32)
         for s in range(GROUP):
@@ -215,12 +247,12 @@
         label = jnp.zeros((1, PW), F32)
         for s in range(GROUP):
             t = g * GROUP + s
-            code = band_s[0, t] * BLOBS + (blob_s[0, t] & (BLOBS - 1)) + 1
+            code = (code_s[0, t] & 3) * BLOBS + ((code_s[0, t] >> 2) & (BLOBS - 1)) + 1
             label = jnp.where(lane[0:1] == SLOTS * s, code.astype(F32), label)
         extra = jnp.where(sub == 0, rhs, jnp.where(sub == 1, diag + label, 0.0))
         for s in range(GROUP):
             t = g * GROUP + s
-            zone = blob_s[0, t] >> 6
+            zone = code_s[0, t] >> 8
             place = used[zone]
             used[zone] = place + 1
             shift = SLOTS * (place - s)
@@ -232,17 +264,58 @@
             mine = (spot & 3) == place
             out[zone] = jnp.where(mine, value, out[zone])
 
-    groups = tiles // GROUP
-    render(0, buf_a)
-
-    def step(n, _):
-        render(2 * n + 1, buf_b)
-        finish(2 * n, buf_a)
-        render(jnp.minimum(2 * n + 2, groups - 1), buf_a)
-        finish(2 * n + 1, buf_b)
-        return 0
-
-    lax.fori_loop(0, groups // 2, step, 0)
+    def run(sum_a, sum_b, rhs_a, rhs_b):
+        def load(buf, k, unit, stage):
+            pltpu.matmul_push_rhs(buf[k, 0:256, :], stage, unit, transpose=True)
+
+        def multiply(g, buf, k, unit, stage):
+            pltpu.matmul_acc_lhs((sum_a, sum_b)[unit], buf[k, 128:256, :], load_staged_rhs=stage)
+            pltpu.matmul_acc_lhs((rhs_a, rhs_b)[unit], scaled[g, k])
+
+        def total():
+            gram = pltpu.matmul_pop(sum_a) + pltpu.matmul_pop(sum_b)
+            return gram, pltpu.matmul_pop(rhs_a) + pltpu.matmul_pop(rhs_b)
+
+        def both(g, buf, before):
+
+            def pair(u, _):
+                steps = [{}, {}]
+                if before is not None:
+                    for stage in range(2):
+                        for unit in range(2):
+                            work = (4 * u + 2 * stage + unit, unit, stage)
+                            n = 2 * (2 * stage + unit) + 1
+                            steps[0][n] = functools.partial(load, before[1], *work)
+                            n = 8 * (1 - stage) + 2 * unit + 1
+                            steps[stage][n] = functools.partial(multiply, *before, *work)
+                for half in range(2):
+                    render(g, 2 * u + half, buf, steps[half])
+                return 0
+
+            lax.fori_loop(0, GROUP // 2, pair, 0, unroll=2)
+            if before is not None:
+                finish(before[0], *total())
+
+        def last(g, buf):
+            for k in range(2 * GROUP):
+                load(buf, k, k % 2, k // 2 % 2)
+                multiply(g, buf, k, k % 2, k // 2 % 2)
+            finish(g, *total())
+
+        groups = tiles // GROUP
+        both(0, buf_a, None)
+
+        def step(n, _):
+            both(2 * n + 1, buf_b, (2 * n, buf_a))
+            both(2 * n + 2, buf_a, (2 * n + 1, buf_b))
+            return 0
+
+        lax.fori_loop(0, groups // 2 - 1, step, 0)
+        both(groups - 1, buf_b, (groups - 2, buf_a))
+        last(groups - 1, buf_b)
+
+    shapes = [pltpu.ACC(unit)((rows, 256), F32) for rows in (128, 16) for unit in range(2)]
+    pl.run_scoped(run, *shapes)
 
 
 def gather_kernel(got, out):
@@ -263,18 +336,22 @@
         body.append(jnp.concatenate([main, extra], axis=1))
     values = jnp.concatenate(body, axis=0)
     label = values[:, PW + SLOTS : PW + SLOTS + 1]
-    systems = out.shape[1]
+    systems = 2 * PW
     codes = iota((4 * zones, systems), 1).astype(F32) + 1.0
     onehot = jnp.where(label == codes, 1.0, 0.0).astype(BF16)
     total = exact_left(values, onehot, TN)
-    out[...] = total[0 : out.shape[0]]
+    out[0:160] = total[0:160, 0:PW]
+    turned = pltpu.roll(total[80:160, PW:systems], EDGE, 1)
+    out[160:240] = jnp.where(iota((80, PW), 1) < EDGE, total[0:80, PW:systems], turned)
 
 
 def solve_kernel(first, second, third, fourth, members, counts, own, before, after, left, right, xs):
-    sums = (first[...] + second[...]) + (third[...] + fourth[...])
-    width = sums.shape[1]
-    left[...] = sums[:, 0:PW]
-    right[...] = sums[:, PW:width]
+    both = (first[...] + second[...]) + (third[...] + fourth[...])
+    width = 2 * PW
+    left[...] = both[0:160]
+    right[0:80] = both[160:240]
+    right[80:160] = pltpu.roll(both[160:240], EDGE, 1)
+    sums = jnp.concatenate([left[...], right[...]], axis=1)
     sub = iota((8, width), 0)
 
     def bcast(x, k):
@@ -341,9 +418,8 @@
         pieces.append(piece)
     flat = jnp.concatenate(pieces, axis=1)
     extent = SRC + 2 * EDGE
-    columns = members[...].astype(F32)
-    slots = iota((BLOBS, SLOTS), 1).astype(F32)
-    columns = jnp.where(slots < counts[...], columns, -1.0)
+    slots = iota((SLOTS, BLOBS), 0)
+    columns = jnp.transpose(jnp.where(slots < counts[...], members[...], -1).astype(F32))
     targets = iota((BLOBS, extent), 1)
     targets = jnp.where(targets < SRC, targets + EDGE, jnp.where(targets < SRC + EDGE, targets - SRC, targets))
     targets = targets.astype(F32)
@@ -393,38 +469,56 @@
     zones = lax.axis_size("zone")
     bands = lax.axis_size("band")
     shape = jax.ShapeDtypeStruct
-    counts = sources_per_blob.astype(F32)
+    counts = sources_per_blob.reshape(1, -1)
+    members = jnp.transpose(blob_members)
     spread = call(table_kernel, shape((zones, TABLE_ROWS, PW), F32), [VMEM] * 4)(
-        blob_members, counts.reshape(1, -1), source_pos, edge_rows.reshape(1, -1)
+        members, counts, source_pos, edge_rows.reshape(1, -1)
     )
     table = lax.all_to_all(spread, "zone", split_axis=0, concat_axis=0, tiled=True)
+    tiles = pixels.shape[0]
+    groups = tiles // GROUP
+    steps = 4
+    rows = pl.BlockSpec((tiles * PH // steps, PW), lambda n: (n, 0))
+    roots, scaled = pl.pallas_call(
+        prepare_kernel,
+        grid=(steps,),
+        out_shape=(
+            shape((tiles * PH, PW), F32),
+            shape((groups, PH // 2, 2 * GROUP, 2 * PW), BF16),
+        ),
+        in_specs=[rows, rows],
+        out_specs=(
+            rows,
+            pl.BlockSpec((groups // steps, PH // 2, 2 * GROUP, 2 * PW), lambda n: (n, 0, 0, 0)),
+        ),
+        compiler_params=pltpu.CompilerParams(vmem_limit_bytes=48 * 1024 * 1024),
+    )(pixels.reshape(tiles * PH, PW), inv_var.reshape(tiles * PH, PW))
     inverse = -LOG2E * (0.5 / (psf_sigma * psf_sigma))
-    tiles = pixels.shape[0]
+    numbers = jnp.concatenate([tile_offset, psf_amp, inverse], axis=0)
+    codes = (tile_blob * 4 + tile_band).reshape(1, -1)
+    places, live_counts = call(
+        place_kernel,
+        (shape((groups, 2 * PW, PW), F32), shape((tiles, PW), F32)),
+        [SMEM, VMEM],
+        [
+            pltpu.VMEM((zones, 8, PW), F32),
+            pltpu.VMEM((tiles, PW), F32),
+            pltpu.VMEM((tiles, 2 * PW), F32),
+        ],
+        (VMEM, VMEM),
+    )(codes, table)
     terms = call(
         tile_kernel,
         shape((zones, 8, PW), F32),
-        [SMEM] * 5 + [VMEM] * 3,
+        [SMEM] * 2 + [VMEM] * 4,
         [
-            pltpu.VMEM((272, PH * PW), BF16),
-            pltpu.VMEM((272, PH * PW), BF16),
-            pltpu.VMEM((GROUP * PH, PW), F32),
-            pltpu.VMEM((zones, 8, PW), F32),
-            pltpu.VMEM((tiles, PW), F32),
-            pltpu.VMEM((tiles, 2 * PW), F32),
+            pltpu.VMEM((PH // 2, 2 * PW, 2 * PW), BF16),
+            pltpu.VMEM((PH // 2, 2 * PW, 2 * PW), BF16),
             pltpu.SMEM((zones,), jnp.int32),
         ],
-    )(
-        tile_blob.reshape(1, -1),
-        tile_band.reshape(1, -1),
-        tile_offset,
-        psf_amp,
-        inverse,
-        table,
-        pixels.reshape(tiles * PH, PW),
-        inv_var.reshape(tiles * PH, PW),
-    )
+    )(codes, numbers, places, live_counts, roots, scaled)
     got = lax.all_to_all(terms, "zone", split_axis=0, concat_axis=0, tiled=True)
-    systems = call(gather_kernel, shape((160, 2 * PW), F32), [VMEM])(got.reshape(zones * 8, PW))
+    systems = call(gather_kernel, shape((240, PW), F32), [VMEM])(got.reshape(zones * 8, PW))
     others = [
         lax.ppermute(systems, "band", [(i, (i + k) % bands) for i in range(bands)])
         for k in range(1, bands)
@@ -435,7 +529,7 @@
         [VMEM] * 6,
         [pltpu.VMEM((160, PW), F32), pltpu.VMEM((160, PW), F32), pltpu.VMEM((SLOTS, 2 * PW), F32)],
         (VMEM, VMEM, VMEM),
-    )(systems, *others, blob_members, counts.reshape(-1, 1))
+    )(systems, *others, members, counts)
     up = [(i, i + 1) for i in range(zones - 1)]
     down = [(b, a) for a, b in up]
     from_before = lax.ppermute(after, "zone", up)

time: 123 us -> 106 us (0.86)
  waiting for transfers between devices: 25 us -> 18.6 us
  Pallas kernels: 43.6 us -> 39.1 us
  local copies, waits for them, and re-layouts: 8.18 us -> 4.18 us
  other arithmetic: 1.35 us -> 0.02 us
    all_to_all x1, waiting for transfers between devices: 15.3 us -> 9.97 us  [on_device(): lax.all_to_all(spread, 'zone', split_axis=0, concat_axis=0, tiled=True)]
    pallas_call x2 -> x4, Pallas kernels: 40.1 us -> 35.6 us  [the longest x1 25.9 us: on_device(): call(tile_kernel, shape((zones, 8, PW), F32), [SMEM] * 2 + [VMEM] * 4, [p...]
    unnamed x19 -> x26, local copies, waits for them, and re-layouts: 7.97 us -> 4.06 us
  transfers between devices with their start and end apart: 6 -> 6, of which waited for: 4 -> 5; matrix products, arithmetic and copies ran while one was open for 1% -> 0% of each run, Pallas kernels for 0% -> 4%
where the time goes in v2:
time: 106 us
  Pallas kernels  39.1 us (37%)
  starting transfers between devices  25.7 us (24%)
  waiting for transfers between devices  18.6 us (18%)
  blocking collectives  18.1 us (17%)
  local copies, waits for them, and re-layouts  4.18 us (4%)
    pallas_call x1, Pallas kernels, on_device(): call(tile_kernel, shape((zones, 8, PW), F32), [SMEM] * 2 + [VMEM] * 4, [p...  25.9 us
    all_to_all x1, blocking collectives, on_device(): got = lax.all_to_all(terms, 'zone', split_axis=0, concat_axis=0, tiled=True)  18.1 us
    all_to_all x1, starting transfers between devices, on_device(): lax.all_to_all(spread, 'zone', split_axis=0, concat_axis=0, tiled=True)  12.2 us
    all_to_all x1, waiting for transfers between devices, on_device(): lax.all_to_all(spread, 'zone', split_axis=0, concat_axis=0, tiled=True)  9.97 us
    ppermute x1, starting transfers between devices, on_device(): from_before = lax.ppermute(after, 'zone', up)  6.73 us
    ppermute x1, waiting for transfers between devices, on_device(): from_after = lax.ppermute(before, 'zone', down)  4.98 us
    ppermute x3, starting transfers between devices, on_device(): lax.ppermute(systems, 'band', [(i, (i + k) % bands) for i in range(bands)])  4.9 us
    pallas_call x1, Pallas kernels, on_device(): pl.pallas_call(prepare_kernel, grid=(steps,), out_shape=(shape((tiles * P...  4.59 us
  transfers between devices with their start and end apart: 6, of which 5 were waited for; matrix products, arithmetic and copies ran while one was open for 0% of the time, Pallas kernels for 4%

profile of v2, /device:TPU:25, one launch (start us, length us, event | category | flops | bytes accessed | tf_op | source)
XLA Modules:
  0.0 105.9 jit_solution(17524551965203665166)
XLA Ops:
  0.0 0.7 copy-done.1
  0.7 0.7 copy-done.3
  1.4 0.7 copy-done.4
  2.0 0.7 copy-done.6
  2.7 1.5 %shard_map.109 = f32[64,16,128]{2,1,0:T(8,128)} custom-call(s32[16,64]{1,0:T(8,128)S(1)} %bitcast.10, s32[1,64]{1,0:T(1,128)S(1)} %bitcast.12, f32[2,512]{1,0:T(2,128)S(1)} %copy-done.3, s32[1,128]{1,0:T(1,128)S(1)} %bitcast.14), custom_call_target="tpu_custom_call" | custom-call | tf_op jit(solution)/shard_map/pallas_call | solution.py:474
  4.2 12.2 %all-to-all-start = ((f32[64,16,128]{2,1,0:T(8,128)}), f32[64,16,128]{2,1,0:T(8,128)S(1)}, u32[]{:S(2)}, u32[]{:S(2)}) async-start(f32[64,16,128]{2,1,0:T(8,128)} %shard_map.109), calls=%async_computation | async-start | bytes 1048576 | tf_op jit(solution)/shard_map/all_to_all | solution.py:477
  16.5 4.6 %shard_map.111 = (f32[4096,128]{1,0:T(8,128)S(1)}, bf16[16,16,16,256]{3,2,1,0:T(8,128)(2,1)S(1)}) custom-call(f32[4096,128]{1,0:T(8,128)} %bitcast.16, f32[4096,128]{1,0:T(8,128)} %bitcast.17), custom_call_target="tpu_custom_call" | custom-call | tf_op jit(solution)/shard_map/pallas_call | solution.py:482
  21.1 1.3 %copy-done = bf16[16,16,16,256]{3,2,1,0:T(8,128)(2,1)} copy-done((bf16[16,16,16,256]{3,2,1,0:T(8,128)(2,1)}, bf16[16,16,16,256]{3,2,1,0:T(8,128)(2,1)S(1)}, u32[]{:S(2)}) %copy-start) | copy-done | bytes 2097176
  22.5 10.0 %all-to-all-done.table = f32[64,16,128]{2,1,0:T(8,128)S(1)} async-done(((f32[64,16,128]{2,1,0:T(8,128)}), f32[64,16,128]{2,1,0:T(8,128)S(1)}, u32[]{:S(2)}, u32[]{:S(2)}) %all-to-all-start) | async-done | bytes 524320 | tf_op jit(solution)/shard_map/all_to_all | solution.py:477
  32.4 4.4 %shard_map.110 = (f32[16,256,128]{2,1,0:T(8,128)S(1)}, f32[128,128]{1,0:T(8,128)S(1)}) custom-call(s32[1,128]{1,0:T(1,128)S(1)} %add_bitcast_fusion.code_s, f32[64,16,128]{2,1,0:T(8,128)S(1)} %all-to-all-done.table), custom_call_target="tpu_custom_call" | custom-call | tf_op jit(solution)/shard_map/pallas_call | solution.py:499
  36.9 25.9 %shard_map.112 = f32[64,8,128]{2,1,0:T(8,128)S(1)} custom-call(s32[1,128]{1,0:T(1,128)S(1)} %add_bitcast_fusion.code_s, f32[8,128]{1,0:T(8,128)S(1)} %pad_maximum_fusion.par_s, f32[16,256,128]{2,1,0:T(8,128)S(1)} %get-tuple-element.12.places, f32[128,128]{1,0:T(8,128)S(1)} %get-tuple-element.13.counts, f32[4096,128]{1,0:T(8,128)S(1)} %get-tuple-element.14.roots, ...), custom_call_target="tpu_custom_call" | custom-call | tf_op jit(solution)/shard_map/pallas_call | solution.py:510
  62.8 18.1 %all_to_all.10 = f32[64,8,128]{2,1,0:T(8,128)S(1)} all-to-all(f32[64,8,128]{2,1,0:T(8,128)S(1)} %shard_map.112), channel_id=1, replica_groups=mesh['zone'=64,'band'=4] {'zone'}, dimensions={0} | all-to-all | bytes 524288 | tf_op jit(solution)/shard_map/all_to_all | solution.py:520
  80.8 0.7 shard_map.113.first
  81.6 1.3 %collective-permute-start = (f32[240,128]{1,0:T(8,128)S(1)}, f32[240,128]{1,0:T(8,128)S(1)}, u32[]{:S(2)}, u32[]{:S(2)}) collective-permute-start(f32[240,128]{1,0:T(8,128)S(1)} %shard_map.113.first), channel_id=1, source_target_pairs={{0,1},{1,2},{2,3},{3,0},{4,5},{5,6},{6,7},{7,4},{8,9},{9,10},{10,1... | collective-permute-start | bytes 368648 | tf_op jit(solution)/shard_map/ppermute | solution.py:523
  82.9 2.4 %collective-permute-start.1 = (f32[240,128]{1,0:T(8,128)S(1)}, f32[240,128]{1,0:T(8,128)S(1)}, u32[]{:S(2)}, u32[]{:S(2)}) collective-permute-start(f32[240,128]{1,0:T(8,128)S(1)} %shard_map.113.first), channel_id=1, source_target_pairs={{0,2},{1,3},{2,0},{3,1},{4,6},{5,7},{6,4},{7,5},{8,10},{9,11},{10,... | collective-permute-start | bytes 368648 | tf_op jit(solution)/shard_map/ppermute | solution.py:523
  85.3 1.2 %collective-permute-start.2 = (f32[240,128]{1,0:T(8,128)S(1)}, f32[240,128]{1,0:T(8,128)S(1)}, u32[]{:S(2)}, u32[]{:S(2)}) collective-permute-start(f32[240,128]{1,0:T(8,128)S(1)} %shard_map.113.first), channel_id=1, source_target_pairs={{0,3},{1,0},{2,1},{3,2},{4,7},{5,4},{6,5},{7,6},{8,11},{9,8},{10,9... | collective-permute-start | bytes 368648 | tf_op jit(solution)/shard_map/ppermute | solution.py:523
  86.5 0.1 collective-permute-done.second
  86.6 2.9 %collective-permute-done.1.third = f32[240,128]{1,0:T(8,128)S(1)} collective-permute-done((f32[240,128]{1,0:T(8,128)S(1)}, f32[240,128]{1,0:T(8,128)S(1)}, u32[]{:S(2)}, u32[]{:S(2)}) %collective-permute-start.1) | collective-permute-done | bytes 122912 | tf_op jit(solution)/shard_map/ppermute | solution.py:523
  89.5 0.6 collective-permute-done.2.fourth
  90.1 1.2 %shard_map.114 = (f32[8,512]{1,0:T(8,128)S(1)}, f32[8,128]{1,0:T(8,128)S(1)}, f32[8,128]{1,0:T(8,128)S(1)}) custom-call(f32[240,128]{1,0:T(8,128)S(1)} %shard_map.113.first, f32[240,128]{1,0:T(8,128)S(1)} %collective-permute-done.second, f32[240,128]{1,0:T(8,128)S(1)} %collective-permute-done.1.third, f32[240,128]{1,0:T(8,128)S(1)} %collective-permute-done.2.fourth, ...), custom_call_target="tpu_custom_call" | custom-call | tf_op jit(solution)/shard_map/pallas_call | solution.py:526
  91.3 6.7 %collective-permute-start.3 = (f32[8,128]{1,0:T(8,128)S(1)}, f32[8,128]{1,0:T(8,128)S(1)}, u32[]{:S(2)}, u32[]{:S(2)}) collective-permute-start(f32[8,128]{1,0:T(8,128)S(1)} %get-tuple-element.17), channel_id=1, source_target_pairs={{0,4},{4,8},{8,12},{12,16},{16,20},{20,24},{24,28},{28,32},{32,36}... | collective-permute-start | bytes 12296 | tf_op jit(solution)/shard_map/ppermute | solution.py:535
  98.1 1.9 %collective-permute-start.4 = (f32[8,128]{1,0:T(8,128)S(1)}, f32[8,128]{1,0:T(8,128)S(1)}, u32[]{:S(2)}, u32[]{:S(2)}) collective-permute-start(f32[8,128]{1,0:T(8,128)S(1)} %get-tuple-element.18), channel_id=1, source_target_pairs={{4,0},{8,4},{12,8},{16,12},{20,16},{24,20},{28,24},{32,28},{36,32}... | collective-permute-start | bytes 12296 | tf_op jit(solution)/shard_map/ppermute | solution.py:536
  100.1 5.0 %collective-permute-done.4.from_after = f32[8,128]{1,0:T(8,128)S(1)} collective-permute-done((f32[8,128]{1,0:T(8,128)S(1)}, f32[8,128]{1,0:T(8,128)S(1)}, u32[]{:S(2)}, u32[]{:S(2)}) %collective-permute-start.4) | collective-permute-done | bytes 4128 | tf_op jit(solution)/shard_map/ppermute | solution.py:536
  105.1 0.8 shard_map.115
  (26 shorter events, 0.2 us)
Async XLA Ops:
  0.0 0.7 copy-start.1
  0.7 0.7 copy-start.3
  1.4 0.7 copy-start.4
  2.0 0.7 copy-start.6
  4.2 28.2 %all-to-all-start = ((f32[64,16,128]{2,1,0:T(8,128)}), f32[64,16,128]{2,1,0:T(8,128)S(1)}, u32[]{:S(2)}, u32[]{:S(2)}) async-start(f32[64,16,128]{2,1,0:T(8,128)} %shard_map.109), calls=%async_computation | async-start | bytes 1048576 | tf_op jit(solution)/shard_map/all_to_all | solution.py:477
  16.4 6.0 %copy-start.8 = (f32[3,128]{1,0:T(4,128)S(1)}, f32[3,128]{1,0:T(4,128)}, u32[]{:S(2)}) copy-start(f32[3,128]{1,0:T(4,128)} %param.15) | copy-start | bytes 4612
  16.4 6.0 %copy-start.9 = (f32[3,128]{1,0:T(4,128)S(1)}, f32[3,128]{1,0:T(4,128)}, u32[]{:S(2)}) copy-start(f32[3,128]{1,0:T(4,128)} %param.14) | copy-start | bytes 4612
  16.4 6.0 %copy-start.10 = (f32[2,128]{1,0:T(2,128)S(1)}, f32[2,128]{1,0:T(2,128)}, u32[]{:S(2)}) copy-start(f32[2,128]{1,0:T(2,128)} %param.13) | copy-start | bytes 3076
  16.4 6.0 %copy-start.11 = (s32[128]{0:T(128)S(1)}, s32[128]{0:T(128)}, u32[]{:S(2)}) copy-start(s32[128]{0:T(128)} %param.17) | copy-start | bytes 1540
  16.4 6.0 %copy-start.12 = (s32[128]{0:T(128)S(1)}, s32[128]{0:T(128)}, u32[]{:S(2)}) copy-start(s32[128]{0:T(128)} %param.16) | copy-start | bytes 1540
  21.1 1.3 %copy-start = (bf16[16,16,16,256]{3,2,1,0:T(8,128)(2,1)}, bf16[16,16,16,256]{3,2,1,0:T(8,128)(2,1)S(1)}, u32[]{:S(2)}) copy-start(bf16[16,16,16,256]{3,2,1,0:T(8,128)(2,1)S(1)} %get-tuple-element.15.scaled) | copy-start | bytes 6291460
  36.8 53.3 %copy-start.2 = (s32[64,16]{0,1:T(8,128)S(1)}, s32[64,16]{0,1:T(8,128)}, u32[]{:S(2)}) copy-start(s32[64,16]{0,1:T(8,128)} %param.20) | copy-start | bytes 12292
  36.8 53.3 %copy-start.5 = (s32[64]{0:T(128)S(1)}, s32[64]{0:T(128)}, u32[]{:S(2)}) copy-start(s32[64]{0:T(128)} %param.21) | copy-start | bytes 772
  36.8 63.1 %copy-start.7 = (s32[128]{0:T(128)S(1)}, s32[128]{0:T(128)}, u32[]{:S(2)}) copy-start(s32[128]{0:T(128)} %param.19) | copy-start | bytes 1540
  81.6 5.0 %collective-permute-start = (f32[240,128]{1,0:T(8,128)S(1)}, f32[240,128]{1,0:T(8,128)S(1)}, u32[]{:S(2)}, u32[]{:S(2)}) collective-permute-start(f32[240,128]{1,0:T(8,128)S(1)} %shard_map.113.first), channel_id=1, source_target_pairs={{0,1},{1,2},{2,3},{3,0},{4,5},{5,6},{6,7},{7,4},{8,9},{9,10},{10,1... | collective-permute-start | bytes 368648 | tf_op jit(solution)/shard_map/ppermute | solution.py:523
  82.9 6.7 %collective-permute-start.1 = (f32[240,128]{1,0:T(8,128)S(1)}, f32[240,128]{1,0:T(8,128)S(1)}, u32[]{:S(2)}, u32[]{:S(2)}) collective-permute-start(f32[240,128]{1,0:T(8,128)S(1)} %shard_map.113.first), channel_id=1, source_target_pairs={{0,2},{1,3},{2,0},{3,1},{4,6},{5,7},{6,4},{7,5},{8,10},{9,11},{10,... | collective-permute-start | bytes 368648 | tf_op jit(solution)/shard_map/ppermute | solution.py:523
  85.3 4.8 %collective-permute-start.2 = (f32[240,128]{1,0:T(8,128)S(1)}, f32[240,128]{1,0:T(8,128)S(1)}, u32[]{:S(2)}, u32[]{:S(2)}) collective-permute-start(f32[240,128]{1,0:T(8,128)S(1)} %shard_map.113.first), channel_id=1, source_target_pairs={{0,3},{1,0},{2,1},{3,2},{4,7},{5,4},{6,5},{7,6},{8,11},{9,8},{10,9... | collective-permute-start | bytes 368648 | tf_op jit(solution)/shard_map/ppermute | solution.py:523
  91.3 8.8 %collective-permute-start.3 = (f32[8,128]{1,0:T(8,128)S(1)}, f32[8,128]{1,0:T(8,128)S(1)}, u32[]{:S(2)}, u32[]{:S(2)}) collective-permute-start(f32[8,128]{1,0:T(8,128)S(1)} %get-tuple-element.17), channel_id=1, source_target_pairs={{0,4},{4,8},{8,12},{12,16},{16,20},{20,24},{24,28},{28,32},{32,36}... | collective-permute-start | bytes 12296 | tf_op jit(solution)/shard_map/ppermute | solution.py:535
  98.1 7.0 %collective-permute-start.4 = (f32[8,128]{1,0:T(8,128)S(1)}, f32[8,128]{1,0:T(8,128)S(1)}, u32[]{:S(2)}, u32[]{:S(2)}) collective-permute-start(f32[8,128]{1,0:T(8,128)S(1)} %get-tuple-element.18), channel_id=1, source_target_pairs={{4,0},{8,4},{12,8},{16,12},{20,16},{24,20},{28,24},{32,28},{36,32}... | collective-permute-start | bytes 12296 | tf_op jit(solution)/shard_map/ppermute | solution.py:536

commit v3 on v2

--- a/solution.py
+++ b/solution.py
@@ -276,7 +276,7 @@
             gram = pltpu.matmul_pop(sum_a) + pltpu.matmul_pop(sum_b)
             return gram, pltpu.matmul_pop(rhs_a) + pltpu.matmul_pop(rhs_b)
 
-        def both(g, buf, before):
+        def both(g, buf, before, done):
 
             def pair(u, _):
                 steps = [{}, {}]
@@ -292,9 +292,10 @@
                     render(g, 2 * u + half, buf, steps[half])
                 return 0
 
-            lax.fori_loop(0, GROUP // 2, pair, 0, unroll=2)
-            if before is not None:
-                finish(before[0], *total())
+            if done is not None:
+                finish(done, *total())
+            pair(jnp.int32(0), 0)
+            lax.fori_loop(1, GROUP // 2, pair, 0)
 
         def last(g, buf):
             for k in range(2 * GROUP):
@@ -303,15 +304,16 @@
             finish(g, *total())
 
         groups = tiles // GROUP
-        both(0, buf_a, None)
+        both(0, buf_a, None, None)
+        both(1, buf_b, (0, buf_a), None)
 
         def step(n, _):
-            both(2 * n + 1, buf_b, (2 * n, buf_a))
-            both(2 * n + 2, buf_a, (2 * n + 1, buf_b))
+            both(2 * n, buf_a, (2 * n - 1, buf_b), 2 * n - 2)
+            both(2 * n + 1, buf_b, (2 * n, buf_a), 2 * n - 1)
             return 0
 
-        lax.fori_loop(0, groups // 2 - 1, step, 0)
-        both(groups - 1, buf_b, (groups - 2, buf_a))
+        lax.fori_loop(1, groups // 2, step, 0)
+        finish(groups - 2, *total())
         last(groups - 1, buf_b)
 
     shapes = [pltpu.ACC(unit)((rows, 256), F32) for rows in (128, 16) for unit in range(2)]

time: 106 us -> 105 us (level)
  Pallas kernels: 39.1 us -> 37.3 us
    pallas_call x1, Pallas kernels: 25.9 us -> 24.1 us  [on_device(): call(tile_kernel, shape((zones, 8, PW), F32), [SMEM] * 2 + [VMEM] * 4, [p...]
where the time goes in v3:
time: 105 us; the launch traced here: 104 us
  Pallas kernels  37.3 us (36%)
  starting transfers between devices  25.8 us (25%)
  waiting for transfers between devices  18.6 us (18%)
  blocking collectives  18 us (17%)
  local copies, waits for them, and re-layouts  4.18 us (4%)
    pallas_call x1, Pallas kernels, on_device(): call(tile_kernel, shape((zones, 8, PW), F32), [SMEM] * 2 + [VMEM] * 4, [p...  24.1 us
    all_to_all x1, blocking collectives, on_device(): got = lax.all_to_all(terms, 'zone', split_axis=0, concat_axis=0, tiled=True)  18 us
    all_to_all x1, starting transfers between devices, on_device(): lax.all_to_all(spread, 'zone', split_axis=0, concat_axis=0, tiled=True)  12.2 us
    all_to_all x1, waiting for transfers between devices, on_device(): lax.all_to_all(spread, 'zone', split_axis=0, concat_axis=0, tiled=True)  9.97 us
    ppermute x1, starting transfers between devices, on_device(): from_before = lax.ppermute(after, 'zone', up)  6.74 us
    ppermute x1, waiting for transfers between devices, on_device(): from_after = lax.ppermute(before, 'zone', down)  4.98 us
    ppermute x3, starting transfers between devices, on_device(): lax.ppermute(systems, 'band', [(i, (i + k) % bands) for i in range(bands)])  4.9 us
    pallas_call x1, Pallas kernels, on_device(): pl.pallas_call(prepare_kernel, grid=(steps,), out_shape=(shape((tiles * P...  4.59 us
  transfers between devices with their start and end apart: 6, of which 5 were waited for; matrix products, arithmetic and copies ran while one was open for 0% of the time, Pallas kernels for 4%

profile of v3, /device:TPU:25, one launch (start us, length us, event | category | flops | bytes accessed | tf_op | source)
XLA Modules:
  0.0 104.1 jit_solution(7319236475753544258)
XLA Ops:
  0.0 0.7 copy-done.1
  0.7 0.7 copy-done.3
  1.4 0.7 copy-done.4
  2.0 0.7 copy-done.6
  2.7 1.5 %shard_map.109 = f32[64,16,128]{2,1,0:T(8,128)} custom-call(s32[16,64]{1,0:T(8,128)S(1)} %bitcast.10, s32[1,64]{1,0:T(1,128)S(1)} %bitcast.12, f32[2,512]{1,0:T(2,128)S(1)} %copy-done.3, s32[1,128]{1,0:T(1,128)S(1)} %bitcast.14), custom_call_target="tpu_custom_call" | custom-call | tf_op jit(solution)/shard_map/pallas_call | solution.py:476
  4.2 12.2 %all-to-all-start = ((f32[64,16,128]{2,1,0:T(8,128)}), f32[64,16,128]{2,1,0:T(8,128)S(1)}, u32[]{:S(2)}, u32[]{:S(2)}) async-start(f32[64,16,128]{2,1,0:T(8,128)} %shard_map.109), calls=%async_computation | async-start | bytes 1048576 | tf_op jit(solution)/shard_map/all_to_all | solution.py:479
  16.5 4.6 %shard_map.111 = (f32[4096,128]{1,0:T(8,128)S(1)}, bf16[16,16,16,256]{3,2,1,0:T(8,128)(2,1)S(1)}) custom-call(f32[4096,128]{1,0:T(8,128)} %bitcast.16, f32[4096,128]{1,0:T(8,128)} %bitcast.17), custom_call_target="tpu_custom_call" | custom-call | tf_op jit(solution)/shard_map/pallas_call | solution.py:484
  21.1 1.3 %copy-done = bf16[16,16,16,256]{3,2,1,0:T(8,128)(2,1)} copy-done((bf16[16,16,16,256]{3,2,1,0:T(8,128)(2,1)}, bf16[16,16,16,256]{3,2,1,0:T(8,128)(2,1)S(1)}, u32[]{:S(2)}) %copy-start) | copy-done | bytes 2097176
  22.5 10.0 %all-to-all-done.table = f32[64,16,128]{2,1,0:T(8,128)S(1)} async-done(((f32[64,16,128]{2,1,0:T(8,128)}), f32[64,16,128]{2,1,0:T(8,128)S(1)}, u32[]{:S(2)}, u32[]{:S(2)}) %all-to-all-start) | async-done | bytes 524320 | tf_op jit(solution)/shard_map/all_to_all | solution.py:479
  32.4 4.4 %shard_map.110 = (f32[16,256,128]{2,1,0:T(8,128)S(1)}, f32[128,128]{1,0:T(8,128)S(1)}) custom-call(s32[1,128]{1,0:T(1,128)S(1)} %add_bitcast_fusion.code_s, f32[64,16,128]{2,1,0:T(8,128)S(1)} %all-to-all-done.table), custom_call_target="tpu_custom_call" | custom-call | tf_op jit(solution)/shard_map/pallas_call | solution.py:501
  36.9 24.1 %shard_map.112 = f32[64,8,128]{2,1,0:T(8,128)S(1)} custom-call(s32[1,128]{1,0:T(1,128)S(1)} %add_bitcast_fusion.code_s, f32[8,128]{1,0:T(8,128)S(1)} %pad_maximum_fusion.par_s, f32[16,256,128]{2,1,0:T(8,128)S(1)} %get-tuple-element.12.places, f32[128,128]{1,0:T(8,128)S(1)} %get-tuple-element.13.counts, f32[4096,128]{1,0:T(8,128)S(1)} %get-tuple-element.14.roots, ...), custom_call_target="tpu_custom_call" | custom-call | tf_op jit(solution)/shard_map/pallas_call | solution.py:512
  61.0 18.0 %all_to_all.10 = f32[64,8,128]{2,1,0:T(8,128)S(1)} all-to-all(f32[64,8,128]{2,1,0:T(8,128)S(1)} %shard_map.112), channel_id=1, replica_groups=mesh['zone'=64,'band'=4] {'zone'}, dimensions={0} | all-to-all | bytes 524288 | tf_op jit(solution)/shard_map/all_to_all | solution.py:522
  79.0 0.7 shard_map.113.first
  79.8 1.3 %collective-permute-start = (f32[240,128]{1,0:T(8,128)S(1)}, f32[240,128]{1,0:T(8,128)S(1)}, u32[]{:S(2)}, u32[]{:S(2)}) collective-permute-start(f32[240,128]{1,0:T(8,128)S(1)} %shard_map.113.first), channel_id=1, source_target_pairs={{0,1},{1,2},{2,3},{3,0},{4,5},{5,6},{6,7},{7,4},{8,9},{9,10},{10,1... | collective-permute-start | bytes 368648 | tf_op jit(solution)/shard_map/ppermute | solution.py:525
  81.1 2.4 %collective-permute-start.1 = (f32[240,128]{1,0:T(8,128)S(1)}, f32[240,128]{1,0:T(8,128)S(1)}, u32[]{:S(2)}, u32[]{:S(2)}) collective-permute-start(f32[240,128]{1,0:T(8,128)S(1)} %shard_map.113.first), channel_id=1, source_target_pairs={{0,2},{1,3},{2,0},{3,1},{4,6},{5,7},{6,4},{7,5},{8,10},{9,11},{10,... | collective-permute-start | bytes 368648 | tf_op jit(solution)/shard_map/ppermute | solution.py:525
  83.5 1.2 %collective-permute-start.2 = (f32[240,128]{1,0:T(8,128)S(1)}, f32[240,128]{1,0:T(8,128)S(1)}, u32[]{:S(2)}, u32[]{:S(2)}) collective-permute-start(f32[240,128]{1,0:T(8,128)S(1)} %shard_map.113.first), channel_id=1, source_target_pairs={{0,3},{1,0},{2,1},{3,2},{4,7},{5,4},{6,5},{7,6},{8,11},{9,8},{10,9... | collective-permute-start | bytes 368648 | tf_op jit(solution)/shard_map/ppermute | solution.py:525
  84.8 2.9 %collective-permute-done.1.third = f32[240,128]{1,0:T(8,128)S(1)} collective-permute-done((f32[240,128]{1,0:T(8,128)S(1)}, f32[240,128]{1,0:T(8,128)S(1)}, u32[]{:S(2)}, u32[]{:S(2)}) %collective-permute-start.1) | collective-permute-done | bytes 122912 | tf_op jit(solution)/shard_map/ppermute | solution.py:525
  87.7 0.6 collective-permute-done.2.fourth
  88.3 1.2 %shard_map.114 = (f32[8,512]{1,0:T(8,128)S(1)}, f32[8,128]{1,0:T(8,128)S(1)}, f32[8,128]{1,0:T(8,128)S(1)}) custom-call(f32[240,128]{1,0:T(8,128)S(1)} %shard_map.113.first, f32[240,128]{1,0:T(8,128)S(1)} %collective-permute-done.second, f32[240,128]{1,0:T(8,128)S(1)} %collective-permute-done.1.third, f32[240,128]{1,0:T(8,128)S(1)} %collective-permute-done.2.fourth, ...), custom_call_target="tpu_custom_call" | custom-call | tf_op jit(solution)/shard_map/pallas_call | solution.py:528
  89.5 6.7 %collective-permute-start.3 = (f32[8,128]{1,0:T(8,128)S(1)}, f32[8,128]{1,0:T(8,128)S(1)}, u32[]{:S(2)}, u32[]{:S(2)}) collective-permute-start(f32[8,128]{1,0:T(8,128)S(1)} %get-tuple-element.17), channel_id=1, source_target_pairs={{0,4},{4,8},{8,12},{12,16},{16,20},{20,24},{24,28},{28,32},{32,36}... | collective-permute-start | bytes 12296 | tf_op jit(solution)/shard_map/ppermute | solution.py:537
  96.3 1.9 %collective-permute-start.4 = (f32[8,128]{1,0:T(8,128)S(1)}, f32[8,128]{1,0:T(8,128)S(1)}, u32[]{:S(2)}, u32[]{:S(2)}) collective-permute-start(f32[8,128]{1,0:T(8,128)S(1)} %get-tuple-element.18), channel_id=1, source_target_pairs={{4,0},{8,4},{12,8},{16,12},{20,16},{24,20},{28,24},{32,28},{36,32}... | collective-permute-start | bytes 12296 | tf_op jit(solution)/shard_map/ppermute | solution.py:538
  98.2 0.1 copy.12.edge_rows
  98.3 5.0 %collective-permute-done.4.from_after = f32[8,128]{1,0:T(8,128)S(1)} collective-permute-done((f32[8,128]{1,0:T(8,128)S(1)}, f32[8,128]{1,0:T(8,128)S(1)}, u32[]{:S(2)}, u32[]{:S(2)}) %collective-permute-start.4) | collective-permute-done | bytes 4128 | tf_op jit(solution)/shard_map/ppermute | solution.py:538
  103.3 0.8 shard_map.115
  (26 shorter events, 0.2 us)
Async XLA Ops:
  0.0 0.7 copy-start.1
  0.7 0.7 copy-start.3
  1.4 0.7 copy-start.4
  2.0 0.7 copy-start.6
  4.2 28.2 %all-to-all-start = ((f32[64,16,128]{2,1,0:T(8,128)}), f32[64,16,128]{2,1,0:T(8,128)S(1)}, u32[]{:S(2)}, u32[]{:S(2)}) async-start(f32[64,16,128]{2,1,0:T(8,128)} %shard_map.109), calls=%async_computation | async-start | bytes 1048576 | tf_op jit(solution)/shard_map/all_to_all | solution.py:479
  16.4 6.0 %copy-start.8 = (f32[3,128]{1,0:T(4,128)S(1)}, f32[3,128]{1,0:T(4,128)}, u32[]{:S(2)}) copy-start(f32[3,128]{1,0:T(4,128)} %param.15) | copy-start | bytes 4612
  16.4 6.0 %copy-start.9 = (f32[3,128]{1,0:T(4,128)S(1)}, f32[3,128]{1,0:T(4,128)}, u32[]{:S(2)}) copy-start(f32[3,128]{1,0:T(4,128)} %param.14) | copy-start | bytes 4612
  16.4 6.0 %copy-start.10 = (f32[2,128]{1,0:T(2,128)S(1)}, f32[2,128]{1,0:T(2,128)}, u32[]{:S(2)}) copy-start(f32[2,128]{1,0:T(2,128)} %param.13) | copy-start | bytes 3076
  16.4 6.0 %copy-start.11 = (s32[128]{0:T(128)S(1)}, s32[128]{0:T(128)}, u32[]{:S(2)}) copy-start(s32[128]{0:T(128)} %param.17) | copy-start | bytes 1540
  16.4 6.0 %copy-start.12 = (s32[128]{0:T(128)S(1)}, s32[128]{0:T(128)}, u32[]{:S(2)}) copy-start(s32[128]{0:T(128)} %param.16) | copy-start | bytes 1540
  21.1 1.3 %copy-start = (bf16[16,16,16,256]{3,2,1,0:T(8,128)(2,1)}, bf16[16,16,16,256]{3,2,1,0:T(8,128)(2,1)S(1)}, u32[]{:S(2)}) copy-start(bf16[16,16,16,256]{3,2,1,0:T(8,128)(2,1)S(1)} %get-tuple-element.15.scaled) | copy-start | bytes 6291460
  36.8 51.5 %copy-start.2 = (s32[64,16]{0,1:T(8,128)S(1)}, s32[64,16]{0,1:T(8,128)}, u32[]{:S(2)}) copy-start(s32[64,16]{0,1:T(8,128)} %param.20) | copy-start | bytes 12292
  36.8 51.5 %copy-start.5 = (s32[64]{0:T(128)S(1)}, s32[64]{0:T(128)}, u32[]{:S(2)}) copy-start(s32[64]{0:T(128)} %param.21) | copy-start | bytes 772
  36.8 61.3 %copy-start.7 = (s32[128]{0:T(128)S(1)}, s32[128]{0:T(128)}, u32[]{:S(2)}) copy-start(s32[128]{0:T(128)} %param.19) | copy-start | bytes 1540
  79.8 5.0 %collective-permute-start = (f32[240,128]{1,0:T(8,128)S(1)}, f32[240,128]{1,0:T(8,128)S(1)}, u32[]{:S(2)}, u32[]{:S(2)}) collective-permute-start(f32[240,128]{1,0:T(8,128)S(1)} %shard_map.113.first), channel_id=1, source_target_pairs={{0,1},{1,2},{2,3},{3,0},{4,5},{5,6},{6,7},{7,4},{8,9},{9,10},{10,1... | collective-permute-start | bytes 368648 | tf_op jit(solution)/shard_map/ppermute | solution.py:525
  81.1 6.7 %collective-permute-start.1 = (f32[240,128]{1,0:T(8,128)S(1)}, f32[240,128]{1,0:T(8,128)S(1)}, u32[]{:S(2)}, u32[]{:S(2)}) collective-permute-start(f32[240,128]{1,0:T(8,128)S(1)} %shard_map.113.first), channel_id=1, source_target_pairs={{0,2},{1,3},{2,0},{3,1},{4,6},{5,7},{6,4},{7,5},{8,10},{9,11},{10,... | collective-permute-start | bytes 368648 | tf_op jit(solution)/shard_map/ppermute | solution.py:525
  83.5 4.8 %collective-permute-start.2 = (f32[240,128]{1,0:T(8,128)S(1)}, f32[240,128]{1,0:T(8,128)S(1)}, u32[]{:S(2)}, u32[]{:S(2)}) collective-permute-start(f32[240,128]{1,0:T(8,128)S(1)} %shard_map.113.first), channel_id=1, source_target_pairs={{0,3},{1,0},{2,1},{3,2},{4,7},{5,4},{6,5},{7,6},{8,11},{9,8},{10,9... | collective-permute-start | bytes 368648 | tf_op jit(solution)/shard_map/ppermute | solution.py:525
  89.5 8.8 %collective-permute-start.3 = (f32[8,128]{1,0:T(8,128)S(1)}, f32[8,128]{1,0:T(8,128)S(1)}, u32[]{:S(2)}, u32[]{:S(2)}) collective-permute-start(f32[8,128]{1,0:T(8,128)S(1)} %get-tuple-element.17), channel_id=1, source_target_pairs={{0,4},{4,8},{8,12},{12,16},{16,20},{20,24},{24,28},{28,32},{32,36}... | collective-permute-start | bytes 12296 | tf_op jit(solution)/shard_map/ppermute | solution.py:537
  96.3 7.0 %collective-permute-start.4 = (f32[8,128]{1,0:T(8,128)S(1)}, f32[8,128]{1,0:T(8,128)S(1)}, u32[]{:S(2)}, u32[]{:S(2)}) collective-permute-start(f32[8,128]{1,0:T(8,128)S(1)} %get-tuple-element.18), channel_id=1, source_target_pairs={{4,0},{8,4},{12,8},{16,12},{20,16},{24,20},{28,24},{32,28},{36,32}... | collective-permute-start | bytes 12296 | tf_op jit(solution)/shard_map/ppermute | solution.py:538

commit v4 on v3

--- a/solution.py
+++ b/solution.py
@@ -124,7 +124,7 @@
         full[z] = jnp.where(value >= MARK, found, value)
         return 0
 
-    lax.fori_loop(0, zones, patch, 0, unroll=8)
+    lax.fori_loop(0, zones, patch, 0, unroll=16)
 
     def pick(t, _):
         blob = code_s[0, t] >> 2
@@ -132,11 +132,11 @@
         info[pl.ds(t, 1), :] = jnp.where((lane[0:1] & (BLOBS - 1)) == (blob & (BLOBS - 1)), row, 0.0)
         return 0
 
-    lax.fori_loop(0, tiles, pick, 0, unroll=16)
+    lax.fori_loop(0, tiles, pick, 0, unroll=32)
     half = iota((PW, 2 * PW), 0) // BLOBS == iota((PW, 2 * PW), 1) // PW
     ranges[...] = exact_left(info[...], jnp.where(half, 1.0, 0.0).astype(BF16), NN)
     counts[...] = ranges[:, PW : 2 * PW]
-    ones = jnp.ones((PW, PW), BF16)
+    ones = jnp.ones((3 * PW, PW), BF16)
 
     def positions(g, _):
         picked = [[], []]
@@ -153,10 +153,11 @@
                     row = full[zone, 4 * p + n : 4 * p + n + 1, :]
                     value = jnp.where(hits[n], jnp.broadcast_to(row, (SLOTS, PW)), value)
                 picked[p].append(value)
-        places[g] = exact_left(jnp.concatenate(picked[0] + picked[1], axis=0), ones, NN)
+        parts = three_parts(jnp.concatenate(picked[0] + picked[1], axis=0))
+        places[g] = dot(jnp.concatenate(parts, axis=1), ones, NN)
         return 0
 
-    lax.fori_loop(0, tiles // GROUP, positions, 0, unroll=2)
+    lax.fori_loop(0, tiles // GROUP, positions, 0, unroll=4)
 
 
 def tile_kernel(

time: 105 us -> 103 us (0.981)
    pallas_call x1, Pallas kernels: 4.39 us -> 3.31 us  [on_device(): call(place_kernel, (shape((groups, 2 * PW, PW), F32), shape((tiles, PW),...]
where the time goes in v4:
time: 103 us
  Pallas kernels  36.3 us (35%)
  starting transfers between devices  25.7 us (25%)
  waiting for transfers between devices  18.6 us (18%)
  blocking collectives  18.1 us (18%)
  local copies, waits for them, and re-layouts  4.18 us (4%)
    pallas_call x1, Pallas kernels, on_device(): call(tile_kernel, shape((zones, 8, PW), F32), [SMEM] * 2 + [VMEM] * 4, [p...  24.1 us
    all_to_all x1, blocking collectives, on_device(): got = lax.all_to_all(terms, 'zone', split_axis=0, concat_axis=0, tiled=True)  18.1 us
    all_to_all x1, starting transfers between devices, on_device(): lax.all_to_all(spread, 'zone', split_axis=0, concat_axis=0, tiled=True)  12.2 us
    all_to_all x1, waiting for transfers between devices, on_device(): lax.all_to_all(spread, 'zone', split_axis=0, concat_axis=0, tiled=True)  9.97 us
    ppermute x1, starting transfers between devices, on_device(): from_before = lax.ppermute(after, 'zone', up)  6.74 us
    ppermute x1, waiting for transfers between devices, on_device(): from_after = lax.ppermute(before, 'zone', down)  4.98 us
    ppermute x3, starting transfers between devices, on_device(): lax.ppermute(systems, 'band', [(i, (i + k) % bands) for i in range(bands)])  4.89 us
    pallas_call x1, Pallas kernels, on_device(): pl.pallas_call(prepare_kernel, grid=(steps,), out_shape=(shape((tiles * P...  4.59 us
  transfers between devices with their start and end apart: 6, of which 5 were waited for; matrix products, arithmetic and copies ran while one was open for 0% of the time, Pallas kernels for 4%

profile of v4, /device:TPU:25, one launch (start us, length us, event | category | flops | bytes accessed | tf_op | source)
XLA Modules:
  0.0 103.0 jit_solution(8068116700747477047)
XLA Ops:
  0.0 0.7 copy-done.1
  0.7 0.7 copy-done.3
  1.4 0.7 copy-done.4
  2.0 0.7 copy-done.6
  2.7 1.5 %shard_map.109 = f32[64,16,128]{2,1,0:T(8,128)} custom-call(s32[16,64]{1,0:T(8,128)S(1)} %bitcast.10, s32[1,64]{1,0:T(1,128)S(1)} %bitcast.12, f32[2,512]{1,0:T(2,128)S(1)} %copy-done.3, s32[1,128]{1,0:T(1,128)S(1)} %bitcast.14), custom_call_target="tpu_custom_call" | custom-call | tf_op jit(solution)/shard_map/pallas_call | solution.py:477
  4.2 12.2 %all-to-all-start = ((f32[64,16,128]{2,1,0:T(8,128)}), f32[64,16,128]{2,1,0:T(8,128)S(1)}, u32[]{:S(2)}, u32[]{:S(2)}) async-start(f32[64,16,128]{2,1,0:T(8,128)} %shard_map.109), calls=%async_computation | async-start | bytes 1048576 | tf_op jit(solution)/shard_map/all_to_all | solution.py:480
  16.5 4.6 %shard_map.111 = (f32[4096,128]{1,0:T(8,128)S(1)}, bf16[16,16,16,256]{3,2,1,0:T(8,128)(2,1)S(1)}) custom-call(f32[4096,128]{1,0:T(8,128)} %bitcast.16, f32[4096,128]{1,0:T(8,128)} %bitcast.17), custom_call_target="tpu_custom_call" | custom-call | tf_op jit(solution)/shard_map/pallas_call | solution.py:485
  21.1 1.3 %copy-done = bf16[16,16,16,256]{3,2,1,0:T(8,128)(2,1)} copy-done((bf16[16,16,16,256]{3,2,1,0:T(8,128)(2,1)}, bf16[16,16,16,256]{3,2,1,0:T(8,128)(2,1)S(1)}, u32[]{:S(2)}) %copy-start) | copy-done | bytes 2097176
  22.5 10.0 %all-to-all-done.table = f32[64,16,128]{2,1,0:T(8,128)S(1)} async-done(((f32[64,16,128]{2,1,0:T(8,128)}), f32[64,16,128]{2,1,0:T(8,128)S(1)}, u32[]{:S(2)}, u32[]{:S(2)}) %all-to-all-start) | async-done | bytes 524320 | tf_op jit(solution)/shard_map/all_to_all | solution.py:480
  32.4 3.3 %shard_map.110 = (f32[16,256,128]{2,1,0:T(8,128)S(1)}, f32[128,128]{1,0:T(8,128)S(1)}) custom-call(s32[1,128]{1,0:T(1,128)S(1)} %add_bitcast_fusion.code_s, f32[64,16,128]{2,1,0:T(8,128)S(1)} %all-to-all-done.table), custom_call_target="tpu_custom_call" | custom-call | tf_op jit(solution)/shard_map/pallas_call | solution.py:502
  35.8 24.1 %shard_map.112 = f32[64,8,128]{2,1,0:T(8,128)S(1)} custom-call(s32[1,128]{1,0:T(1,128)S(1)} %add_bitcast_fusion.code_s, f32[8,128]{1,0:T(8,128)S(1)} %pad_maximum_fusion.par_s, f32[16,256,128]{2,1,0:T(8,128)S(1)} %get-tuple-element.12.places, f32[128,128]{1,0:T(8,128)S(1)} %get-tuple-element.13.counts, f32[4096,128]{1,0:T(8,128)S(1)} %get-tuple-element.14.roots, ...), custom_call_target="tpu_custom_call" | custom-call | tf_op jit(solution)/shard_map/pallas_call | solution.py:513
  59.9 18.1 %all_to_all.10 = f32[64,8,128]{2,1,0:T(8,128)S(1)} all-to-all(f32[64,8,128]{2,1,0:T(8,128)S(1)} %shard_map.112), channel_id=1, replica_groups=mesh['zone'=64,'band'=4] {'zone'}, dimensions={0} | all-to-all | bytes 524288 | tf_op jit(solution)/shard_map/all_to_all | solution.py:523
  78.0 0.7 shard_map.113.first
  78.7 1.3 %collective-permute-start = (f32[240,128]{1,0:T(8,128)S(1)}, f32[240,128]{1,0:T(8,128)S(1)}, u32[]{:S(2)}, u32[]{:S(2)}) collective-permute-start(f32[240,128]{1,0:T(8,128)S(1)} %shard_map.113.first), channel_id=1, source_target_pairs={{0,1},{1,2},{2,3},{3,0},{4,5},{5,6},{6,7},{7,4},{8,9},{9,10},{10,1... | collective-permute-start | bytes 368648 | tf_op jit(solution)/shard_map/ppermute | solution.py:526
  80.0 2.4 %collective-permute-start.1 = (f32[240,128]{1,0:T(8,128)S(1)}, f32[240,128]{1,0:T(8,128)S(1)}, u32[]{:S(2)}, u32[]{:S(2)}) collective-permute-start(f32[240,128]{1,0:T(8,128)S(1)} %shard_map.113.first), channel_id=1, source_target_pairs={{0,2},{1,3},{2,0},{3,1},{4,6},{5,7},{6,4},{7,5},{8,10},{9,11},{10,... | collective-permute-start | bytes 368648 | tf_op jit(solution)/shard_map/ppermute | solution.py:526
  82.4 1.2 %collective-permute-start.2 = (f32[240,128]{1,0:T(8,128)S(1)}, f32[240,128]{1,0:T(8,128)S(1)}, u32[]{:S(2)}, u32[]{:S(2)}) collective-permute-start(f32[240,128]{1,0:T(8,128)S(1)} %shard_map.113.first), channel_id=1, source_target_pairs={{0,3},{1,0},{2,1},{3,2},{4,7},{5,4},{6,5},{7,6},{8,11},{9,8},{10,9... | collective-permute-start | bytes 368648 | tf_op jit(solution)/shard_map/ppermute | solution.py:526
  83.6 0.1 collective-permute-done.second
  83.7 2.9 %collective-permute-done.1.third = f32[240,128]{1,0:T(8,128)S(1)} collective-permute-done((f32[240,128]{1,0:T(8,128)S(1)}, f32[240,128]{1,0:T(8,128)S(1)}, u32[]{:S(2)}, u32[]{:S(2)}) %collective-permute-start.1) | collective-permute-done | bytes 122912 | tf_op jit(solution)/shard_map/ppermute | solution.py:526
  86.6 0.6 collective-permute-done.2.fourth
  87.3 1.2 %shard_map.114 = (f32[8,512]{1,0:T(8,128)S(1)}, f32[8,128]{1,0:T(8,128)S(1)}, f32[8,128]{1,0:T(8,128)S(1)}) custom-call(f32[240,128]{1,0:T(8,128)S(1)} %shard_map.113.first, f32[240,128]{1,0:T(8,128)S(1)} %collective-permute-done.second, f32[240,128]{1,0:T(8,128)S(1)} %collective-permute-done.1.third, f32[240,128]{1,0:T(8,128)S(1)} %collective-permute-done.2.fourth, ...), custom_call_target="tpu_custom_call" | custom-call | tf_op jit(solution)/shard_map/pallas_call | solution.py:529
  88.4 6.7 %collective-permute-start.3 = (f32[8,128]{1,0:T(8,128)S(1)}, f32[8,128]{1,0:T(8,128)S(1)}, u32[]{:S(2)}, u32[]{:S(2)}) collective-permute-start(f32[8,128]{1,0:T(8,128)S(1)} %get-tuple-element.17), channel_id=1, source_target_pairs={{0,4},{4,8},{8,12},{12,16},{16,20},{20,24},{24,28},{28,32},{32,36}... | collective-permute-start | bytes 12296 | tf_op jit(solution)/shard_map/ppermute | solution.py:538
  95.2 1.9 %collective-permute-start.4 = (f32[8,128]{1,0:T(8,128)S(1)}, f32[8,128]{1,0:T(8,128)S(1)}, u32[]{:S(2)}, u32[]{:S(2)}) collective-permute-start(f32[8,128]{1,0:T(8,128)S(1)} %get-tuple-element.18), channel_id=1, source_target_pairs={{4,0},{8,4},{12,8},{16,12},{20,16},{24,20},{28,24},{32,28},{36,32}... | collective-permute-start | bytes 12296 | tf_op jit(solution)/shard_map/ppermute | solution.py:539
  97.2 5.0 %collective-permute-done.4.from_after = f32[8,128]{1,0:T(8,128)S(1)} collective-permute-done((f32[8,128]{1,0:T(8,128)S(1)}, f32[8,128]{1,0:T(8,128)S(1)}, u32[]{:S(2)}, u32[]{:S(2)}) %collective-permute-start.4) | collective-permute-done | bytes 4128 | tf_op jit(solution)/shard_map/ppermute | solution.py:539
  102.2 0.8 shard_map.115
  (26 shorter events, 0.2 us)
Async XLA Ops:
  0.0 0.7 copy-start.1
  0.7 0.7 copy-start.3
  1.4 0.7 copy-start.4
  2.0 0.7 copy-start.6
  4.2 28.2 %all-to-all-start = ((f32[64,16,128]{2,1,0:T(8,128)}), f32[64,16,128]{2,1,0:T(8,128)S(1)}, u32[]{:S(2)}, u32[]{:S(2)}) async-start(f32[64,16,128]{2,1,0:T(8,128)} %shard_map.109), calls=%async_computation | async-start | bytes 1048576 | tf_op jit(solution)/shard_map/all_to_all | solution.py:480
  16.4 6.0 %copy-start.8 = (f32[3,128]{1,0:T(4,128)S(1)}, f32[3,128]{1,0:T(4,128)}, u32[]{:S(2)}) copy-start(f32[3,128]{1,0:T(4,128)} %param.15) | copy-start | bytes 4612
  16.4 6.0 %copy-start.9 = (f32[3,128]{1,0:T(4,128)S(1)}, f32[3,128]{1,0:T(4,128)}, u32[]{:S(2)}) copy-start(f32[3,128]{1,0:T(4,128)} %param.14) | copy-start | bytes 4612
  16.4 6.0 %copy-start.10 = (f32[2,128]{1,0:T(2,128)S(1)}, f32[2,128]{1,0:T(2,128)}, u32[]{:S(2)}) copy-start(f32[2,128]{1,0:T(2,128)} %param.13) | copy-start | bytes 3076
  16.4 6.0 %copy-start.11 = (s32[128]{0:T(128)S(1)}, s32[128]{0:T(128)}, u32[]{:S(2)}) copy-start(s32[128]{0:T(128)} %param.17) | copy-start | bytes 1540
  16.4 6.0 %copy-start.12 = (s32[128]{0:T(128)S(1)}, s32[128]{0:T(128)}, u32[]{:S(2)}) copy-start(s32[128]{0:T(128)} %param.16) | copy-start | bytes 1540
  21.1 1.3 %copy-start = (bf16[16,16,16,256]{3,2,1,0:T(8,128)(2,1)}, bf16[16,16,16,256]{3,2,1,0:T(8,128)(2,1)S(1)}, u32[]{:S(2)}) copy-start(bf16[16,16,16,256]{3,2,1,0:T(8,128)(2,1)S(1)} %get-tuple-element.15.scaled) | copy-start | bytes 6291460
  35.7 51.5 %copy-start.2 = (s32[64,16]{0,1:T(8,128)S(1)}, s32[64,16]{0,1:T(8,128)}, u32[]{:S(2)}) copy-start(s32[64,16]{0,1:T(8,128)} %param.20) | copy-start | bytes 12292
  35.8 51.5 %copy-start.5 = (s32[64]{0:T(128)S(1)}, s32[64]{0:T(128)}, u32[]{:S(2)}) copy-start(s32[64]{0:T(128)} %param.21) | copy-start | bytes 772
  35.8 61.3 %copy-start.7 = (s32[128]{0:T(128)S(1)}, s32[128]{0:T(128)}, u32[]{:S(2)}) copy-start(s32[128]{0:T(128)} %param.19) | copy-start | bytes 1540
  78.7 5.0 %collective-permute-start = (f32[240,128]{1,0:T(8,128)S(1)}, f32[240,128]{1,0:T(8,128)S(1)}, u32[]{:S(2)}, u32[]{:S(2)}) collective-permute-start(f32[240,128]{1,0:T(8,128)S(1)} %shard_map.113.first), channel_id=1, source_target_pairs={{0,1},{1,2},{2,3},{3,0},{4,5},{5,6},{6,7},{7,4},{8,9},{9,10},{10,1... | collective-permute-start | bytes 368648 | tf_op jit(solution)/shard_map/ppermute | solution.py:526
  80.0 6.7 %collective-permute-start.1 = (f32[240,128]{1,0:T(8,128)S(1)}, f32[240,128]{1,0:T(8,128)S(1)}, u32[]{:S(2)}, u32[]{:S(2)}) collective-permute-start(f32[240,128]{1,0:T(8,128)S(1)} %shard_map.113.first), channel_id=1, source_target_pairs={{0,2},{1,3},{2,0},{3,1},{4,6},{5,7},{6,4},{7,5},{8,10},{9,11},{10,... | collective-permute-start | bytes 368648 | tf_op jit(solution)/shard_map/ppermute | solution.py:526
  82.4 4.8 %collective-permute-start.2 = (f32[240,128]{1,0:T(8,128)S(1)}, f32[240,128]{1,0:T(8,128)S(1)}, u32[]{:S(2)}, u32[]{:S(2)}) collective-permute-start(f32[240,128]{1,0:T(8,128)S(1)} %shard_map.113.first), channel_id=1, source_target_pairs={{0,3},{1,0},{2,1},{3,2},{4,7},{5,4},{6,5},{7,6},{8,11},{9,8},{10,9... | collective-permute-start | bytes 368648 | tf_op jit(solution)/shard_map/ppermute | solution.py:526
  88.4 8.8 %collective-permute-start.3 = (f32[8,128]{1,0:T(8,128)S(1)}, f32[8,128]{1,0:T(8,128)S(1)}, u32[]{:S(2)}, u32[]{:S(2)}) collective-permute-start(f32[8,128]{1,0:T(8,128)S(1)} %get-tuple-element.17), channel_id=1, source_target_pairs={{0,4},{4,8},{8,12},{12,16},{16,20},{20,24},{24,28},{28,32},{32,36}... | collective-permute-start | bytes 12296 | tf_op jit(solution)/shard_map/ppermute | solution.py:538
  95.2 7.0 %collective-permute-start.4 = (f32[8,128]{1,0:T(8,128)S(1)}, f32[8,128]{1,0:T(8,128)S(1)}, u32[]{:S(2)}, u32[]{:S(2)}) collective-permute-start(f32[8,128]{1,0:T(8,128)S(1)} %get-tuple-element.18), channel_id=1, source_target_pairs={{4,0},{8,4},{12,8},{16,12},{20,16},{24,20},{28,24},{32,28},{36,32}... | collective-permute-start | bytes 12296 | tf_op jit(solution)/shard_map/ppermute | solution.py:539
